TPU v7x, 32 devices: a whole 2x2x4 slice. The times are simulated.
32 devices in a mesh: pb: 2 (over y), pool: 4 (over z), ga: 2 (over x), pert: 2 (over core).
Axes of the slice: x: 2, y: 2, z: 4, core: 2. Of those that a mesh axis runs over, the one named last changes fastest.
Arguments:
- wavefunctions: bfloat16 [64, 12, 240, 128], P('pool', 'ga'), may hold values from -6 to 6
- potentials: float32 [12, 12, 240], P(('pb', 'pert'), 'ga'), parts along dimension 0, may hold values from -6 to 6
- pert_order: int32 [6], replicated, may hold values from 0 to 5, each once
- partners: int32 [128], P('pb'), parts along dimension 0, may hold values from 0 to 63, as said below
Outputs:
- couplings: bfloat16 [128, 6, 2, 128, 128], P(('pb', 'pool'), 'pert', None, 'ga'), parts along dimension 0
There are 2 independent parts, one for each index of `pb`. A program takes and returns all parts, laid end to end along the dimension named above; an argument that names none is the same for every part. Nothing has to cross between parts.
Inputs may be any that keep to these rules, and one draw needn't show every extreme that they name: `partners`: A permutation of the 64 k-points; k-point k is owned by pool k // 16. For any two pools (one pool with itself included), at most 5 k-points of the one have their k+q owned by the other, and exactly 5 for some pair in every draw. The numbers of k-points that one pool takes from each pool are the same list for every pool, up to order. `pert_order`: each number once.
All inputs are finite; a program needn't handle non-finite values.
Results may differ from a plain program's by a relative error of at most 0.0073.
Values may be sent and summed in bfloat16 or wider, within the bound.
No kernel may reach another device: no remote copies, remote signals or barrier semaphores. Data moves between devices by JAX's collectives and lax.ppermute only.
A program may use at most 128 MiB of HBM per device.

v0:
```python
import functools
import math

import jax
import jax.numpy as jnp
from jax import lax
from jax.experimental import pallas as pl
from jax.experimental.pallas import tpu as pltpu
from jax.sharding import PartitionSpec as P

BF16 = jnp.bfloat16
F32 = jnp.float32
ANY = pl.BlockSpec(memory_space=pl.ANY)
SMEM = pl.BlockSpec(memory_space=pltpu.SMEM)
VMEM_LIMIT = 60 * 1024 * 1024
LIGHT = pl.CostEstimate(flops=1, bytes_accessed=1024, transcendentals=0)
PARAMS = pltpu.CompilerParams(vmem_limit_bytes=VMEM_LIMIT)


def dft_table(length):
    positions = jnp.arange(length, dtype=jnp.int32)
    product = positions[:, None] * positions[None, :] % length
    angles = product.astype(F32) * (2.0 * math.pi / length)
    cosine = jnp.cos(angles) / math.sqrt(length)
    sine_part = jnp.sin(angles) / math.sqrt(length)
    upper_rows = jnp.concatenate([cosine, -sine_part], axis=1)
    bottom = jnp.concatenate([sine_part, cosine], axis=1)
    return jnp.concatenate([upper_rows, bottom], axis=0).astype(BF16)


def plan_kernel(pools, local_k, cap, ids, partners, plan):
    me = ids[0]
    size = pools * cap
    counts = 3 * size

    def clear(i, carry):
        plan[i] = 0
        return carry

    lax.fori_loop(0, counts + pools, clear, 0, unroll=8)

    def visit(t, tally):
        want = partners[me * local_k + t]
        holder = lax.div(want, local_k)
        shift = lax.rem(me - holder + pools, pools)
        slot = plan[counts + shift]
        plan[shift * cap + slot] = t
        plan[size + shift * cap + slot] = want - holder * local_k
        plan[counts + shift] = slot + 1
        after = []
        for shift in range(1, pools):
            taker = lax.rem(me + shift, pools)
            want = partners[taker * local_k + t]
            slot = tally[shift - 1]
            mine = lax.div(want, local_k) == me
            entry = 2 * size + shift * cap + jnp.minimum(slot, cap - 1)
            plan[entry] = jnp.where(mine, lax.rem(want, local_k), plan[entry])
            after.append(slot + mine.astype(jnp.int32))
        return tuple(after)

    lax.fori_loop(0, local_k, visit, (jnp.int32(0),) * (pools - 1), unroll=2)


def make_plan(ids, partners, pools, local_k, cap):
    return pl.pallas_call(
        functools.partial(plan_kernel, pools, local_k, cap),
        out_shape=jax.ShapeDtypeStruct((3 * pools * cap + pools,), jnp.int32),
        in_specs=[SMEM, SMEM],
        out_specs=SMEM,
        cost_estimate=LIGHT,
        name="plan",
    )(ids, partners)


def pick_kernel(base, plan, ids, waves, give, sems):
    copies = [
        pltpu.make_async_copy(waves.at[plan[base + i] * 2 + ids[1]], give.at[i], sems.at[i])
        for i in range(give.shape[0])
    ]
    for copy in copies:
        copy.start()
    for copy in copies:
        copy.wait()


def pick(plan, ids, waves, pools, cap, chunk):
    shift, first, count = chunk
    return pl.pallas_call(
        functools.partial(pick_kernel, (2 * pools + shift) * cap + first),
        out_shape=jax.ShapeDtypeStruct((count,) + waves.shape[1:], waves.dtype),
        in_specs=[SMEM, SMEM, ANY],
        out_specs=pl.BlockSpec(memory_space=pltpu.VMEM),
        scratch_shapes=[pltpu.SemaphoreType.DMA((count,))],
        compiler_params=PARAMS,
        cost_estimate=LIGHT,
        name="pick",
    )(plan, ids, waves)


def to_real(own, other, table, z_points):
    stacked = 2 * z_points
    bands = own.shape[1]
    parts = [[], [], [], []]
    for c in range(own.shape[0] // stacked):
        rows = slice(c * stacked, (c + 1) * stacked)
        pair = jnp.concatenate([own[rows], other[rows]], axis=1)
        out = jnp.dot(table, pair, preferred_element_type=F32)
        parts[0].append(out[:z_points, :bands])
        parts[1].append(out[z_points:, :bands])
        parts[2].append(out[:z_points, bands:])
        parts[3].append(out[z_points:, bands:])
    return [jnp.concatenate(part, axis=0).astype(BF16) for part in parts]


def piece_of(count):
    return max(1, count // 2)


def couple_kernel(shape, plan, ids, table, pots, own, other, keep, *rest):
    number, first, size, groups, z_points = shape
    gives, hold = rest[:-1], rest[-1]

    @pl.when(first + pl.program_id(0) < plan[number])
    def _():
        own_re, own_im, o_re, o_im = to_real(own[0], other[0], table[...], z_points)
        u_re, u_im = own_re.astype(F32), own_im.astype(F32)
        both_o = jnp.concatenate([o_re, o_im], axis=1).T
        bands = o_re.shape[1]
        share = bands // groups
        mine = pots.shape[0] // 2
        starts = [
            pl.multiple_of(lax.rem(g - ids[2] + groups, groups) * share, share)
            for g in range(groups)
        ]
        for j in range(2 * mine):
            p_re, p_im = pots[j, 0], pots[j, 1]
            w_re = (p_re * u_re - p_im * u_im).astype(BF16)
            w_im = (p_re * u_im + p_im * u_re).astype(BF16)
            both = jnp.dot(
                both_o, jnp.concatenate([w_re, w_im], axis=1), preferred_element_type=F32
            )
            real = both[:bands, :bands] + both[bands:, bands:]
            imag = both[:bands, bands:] - both[bands:, :bands]
            for part, value in ((0, real), (1, imag)):
                for g in range(groups):
                    rows = value[g * share : (g + 1) * share]
                    if j < mine:
                        keep[0, 2 * j + part, pl.ds(starts[g], share), :] = rows
                    else:
                        place = 2 * (j - mine) + part
                        hold[place, pl.ds(starts[g], share), :] = rows.astype(BF16)

        for at, give in enumerate(gives):

            @pl.when(pl.program_id(0) // size == at)
            def _(give=give):
                give[0] = hold[...]


def couple(plan, ids, table, pots, waves, other, chunk, pools, cap, groups):
    shift, first, count = chunk
    half, bands = waves.shape[1:]
    parts = pots.shape[0]
    base = shift * cap + first
    block = (1, half, bands)
    own_block = pl.BlockSpec(block, lambda i, plan, ids: (plan[base + i] * 2 + ids[1], 0, 0))
    if shift == 0:
        other_block = pl.BlockSpec(
            block, lambda i, plan, ids: (plan[pools * cap + base + i] * 2 + ids[1], 0, 0)
        )
    else:
        other_block = pl.BlockSpec(block, lambda i, plan, ids: (i, 0, 0))
    out_block = (1, parts, bands, bands)
    size = piece_of(count)
    pieces = [(at, min(size, count - at)) for at in range(0, count, size)]
    shape = (3 * pools * cap + shift, first, size, groups, table.shape[0] // 2)
    return pl.pallas_call(
        functools.partial(couple_kernel, shape),
        grid_spec=pltpu.PrefetchScalarGridSpec(
            num_scalar_prefetch=2,
            grid=(count,),
            in_specs=[
                pl.BlockSpec(table.shape, lambda i, plan, ids: (0, 0)),
                pl.BlockSpec(pots.shape, lambda i, plan, ids: (0, 0, 0, 0)),
                own_block, other_block,
            ],
            out_specs=[pl.BlockSpec(out_block, lambda i, plan, ids: (i, 0, 0, 0))] + [
                pl.BlockSpec(
                    out_block,
                    lambda i, plan, ids, at=at, size=size: (jnp.clip(i - at, 0, size - 1), 0, 0, 0),
                )
                for at, size in pieces
            ],
            scratch_shapes=[pltpu.VMEM((parts, bands, bands), BF16)],
        ),
        out_shape=[jax.ShapeDtypeStruct((count, parts, bands, bands), F32)] + [
            jax.ShapeDtypeStruct((size, parts, bands, bands), BF16) for _, size in pieces
        ],
        compiler_params=PARAMS,
        cost_estimate=LIGHT,
        name="couple",
    )(plan, ids, table, pots, waves, other)


def combine_kernel(shapes, others, scaling, plan, *refs):
    result, stage, sems = refs[-3:]
    terms = list(refs[-3 - sum(1 + shape[4] + others for shape in shapes) : -3])
    blocks = []
    for number, base, first, count, pieces in shapes:
        kept = terms.pop(0)
        added = [([terms.pop(0) for _ in range(pieces)], piece_of(count))]
        added += [([terms.pop(0)], count) for _ in range(others)]
        for i in range(count):
            blocks.append((number, base + i, first + i, kept, added, i))

    def each(action):
        for at, (number, entry, slot, kept, added, i) in enumerate(blocks):

            @pl.when(slot < plan[number])
            def _(at=at, entry=entry, kept=kept, added=added, i=i):
                copy = pltpu.make_async_copy(stage.at[at], result.at[plan[entry]], sems.at[at])
                action(at, copy, kept, added, i)

    def add(at, copy, kept, added, i):
        value = kept[i]
        for pieces, size in added:
            value = value + pieces[i // size][i % size].astype(F32)
        stage[at] = (value * scaling).astype(BF16)
        copy.start()

    each(add)
    each(lambda at, copy, kept, added, i: copy.wait())


def combine(plan, before, parcels, local_k, pools, cap, scaling):
    terms, shapes, total = [], [], 0
    for (shift, first, count), kept, got, arrived in parcels:
        terms += [kept, *got, *arrived]
        shapes.append((3 * pools * cap + shift, shift * cap + first, first, count, len(got)))
        total += count
        others = len(arrived)
        parts, share, bands = arrived[0].shape[1:]
    blocks = [
        pl.BlockSpec((term.shape[0], parts, share, bands), lambda i, plan: (0, 0, 0, 0))
        for term in terms
    ]
    operands = ([] if before is None else [before]) + terms
    return pl.pallas_call(
        functools.partial(combine_kernel, shapes, others, scaling),
        grid_spec=pltpu.PrefetchScalarGridSpec(
            num_scalar_prefetch=1,
            grid=(1,),
            in_specs=([] if before is None else [ANY]) + blocks,
            out_specs=ANY,
            scratch_shapes=[
                pltpu.VMEM((total, parts, share, bands), BF16),
                pltpu.SemaphoreType.DMA((total,)),
            ],
        ),
        out_shape=jax.ShapeDtypeStruct((local_k, parts, share, bands), BF16),
        input_output_aliases={} if before is None else {1: 0},
        compiler_params=PARAMS,
        cost_estimate=LIGHT,
        name="combine",
    )(plan, *operands)


def after(value, *others):
    return lax.optimization_barrier((value, *others))[0]


def transfers(pools, cap):
    moves = []
    for s in range(1, (pools + 1) // 2):
        moves += [(s, 0, cap), (pools - s, 0, cap)]
    if pools % 2 == 0:
        large = (3 * cap + 2) // 5
        moves += [(pools // 2, 0, large), (pools // 2, large, cap - large)]
    waits = [None] + [max(0, i - 2) for i in range(1, len(moves))]
    return moves, waits


def body(wavefunctions, potentials, pert_order, partners):
    local_k, columns, stacked, bands = wavefunctions.shape
    z_points = stacked // 2
    pools = lax.axis_size("pool")
    groups = lax.axis_size("ga")
    cores = lax.axis_size("pert")
    my_pool = lax.axis_index("pool")
    my_core = lax.axis_index("pert")
    my_group = lax.axis_index("ga")
    cap = max(2, local_k // pools + 1)
    half = columns // cores
    share = bands // groups
    ids = jnp.stack([my_pool, my_core, my_group]).astype(jnp.int32)
    waves = wavefunctions.reshape(local_k * cores, half * stacked, bands)
    swap_cores = [(c, cores - 1 - c) for c in range(cores)]

    plan = make_plan(ids, partners, pools, local_k, cap)
    moves, waits = transfers(pools, cap)
    gives = [pick(plan, ids, waves, pools, cap, move) for move in moves]
    potentials = after(potentials, gives[0])

    per_device = potentials.shape[0]
    by_half = potentials.reshape(per_device, cores, half, stacked)
    mine_now = lax.dynamic_index_in_dim(by_half, my_core, 1, keepdims=False)
    theirs_now = lax.dynamic_index_in_dim(by_half, 1 - my_core, 1, keepdims=False)
    other_pots = lax.ppermute(theirs_now, "pert", swap_cores)
    ordered = jnp.roll(pert_order.reshape(cores, per_device), -my_core, axis=0).reshape(-1)
    stored = jnp.where(
        my_core == 0, jnp.stack([mine_now, other_pots]), jnp.stack([other_pots, mine_now])
    ).reshape((cores * per_device,) + mine_now.shape[1:])
    options = jnp.arange(cores * per_device, dtype=jnp.int32)
    chosen = jnp.sum(
        jnp.where(
            (ordered[:, None] == options[None, :])[:, :, None, None], stored[None],
            jnp.zeros((), F32),
        ),
        axis=1,
    ).reshape(cores * per_device, half, 2, z_points)
    pots = jnp.moveaxis(chosen, 2, 1).reshape(cores * per_device, 2, half * z_points, 1)
    pots = jnp.broadcast_to(pots, pots.shape[:3] + (bands,))
    table = dft_table(z_points)
    scaling = 1.0 / math.sqrt(columns * groups * z_points)

    landed = []
    for move, wait, give in zip(moves, waits, gives):
        if wait is not None:
            give = after(give, landed[wait])
        pairs = [(p, (p + move[0]) % pools) for p in range(pools)]
        landed.append(lax.ppermute(give, "pool", pairs))

    chunks = [((0, 0, cap), waves), *zip(moves, landed)]
    kept, got, terms = [], [], []
    result = None

    def exchange(i):
        sent = []
        size = piece_of(kept[i].shape[0])
        for step in range(1, groups):
            rows = slice(step * share, (step + 1) * share)
            pairs = [(g, (g + step) % groups) for g in range(groups)]
            total = jnp.concatenate(
                [
                    kept[i][at * size : at * size + piece.shape[0], :, rows]
                    + piece[:, :, rows].astype(F32)
                    for at, piece in enumerate(got[i])
                ],
                axis=0,
            )
            sent.append(lax.ppermute(total.astype(BF16), "ga", pairs))
        terms.append(sent)

    finished = 0

    def finish(until, result):
        parcels = [(chunks[i][0], kept[i], got[i], terms[i]) for i in range(finished, until)]
        return combine(plan, result, parcels, local_k, pools, cap, scaling)

    last = len(chunks) - 1
    for i, (chunk, other) in enumerate(chunks):
        if i >= 1:
            other = after(other, kept[i - 1])
        if i >= LAG_CORE:
            exchange(i - LAG_CORE)
            other = after(other, *got[i - LAG_CORE])
        if i >= LAG_GROUP:
            other = after(other, *terms[i - LAG_GROUP])
        if last - i in COMBINE and i - LAG_GROUP + 1 > finished:
            result = finish(i - LAG_GROUP + 1, result)
            finished = i - LAG_GROUP + 1
            other = after(other, result)
        keep, *gives_now = couple(plan, ids, table, pots, waves, other, chunk, pools, cap, groups)
        kept.append(keep)
        if i >= last - 1:
            gives_now[-1] = after(gives_now[-1], *terms[i - 1])
        if i == last - 1:
            gives_now[-1] = after(gives_now[-1], landed[-1])
        got.append([lax.ppermute(give, "pert", swap_cores) for give in gives_now])
    for i in range(len(terms), len(chunks)):
        exchange(i)
    result = finish(len(chunks), result)
    return result.reshape(local_k, per_device, 2, share, bands)


LAG_CORE, LAG_GROUP = 1, 2
COMBINE = (1,)


def solution(mesh):
    return jax.shard_map(
        body,
        mesh=mesh,
        in_specs=(P("pool", "ga", None, None), P(("pb", "pert"), "ga", None), P(), P("pb")),
        out_specs=P(("pb", "pool"), "pert", None, "ga", None),
        check_vma=False,
    )
```

profile of v0, /device:TPU:0, one launch (start us, length us, event | category | flops | bytes accessed | tf_op | source)
XLA Modules:
  0.0 118.4 jit_solution(12919563422640604661)
XLA Ops:
  0.7 1.8 %plan.1 = s32[64]{0:T(128)} custom-call(s32[3]{0:T(128)} %pad_add_fusion.1.ids, s32[64]{0:T(128)} %partners.1), custom_call_target="tpu_custom_call" | custom-call | flops 1 | bytes 1024 | tf_op jit(solution)/shard_map/plan/pallas_call | solution.py:65
  2.5 3.0 %pick.4 = bf16[5,720,128]{2,1,0:T(8,128)(2,1)} custom-call(s32[64]{0:T(128)} %plan.1, s32[3]{0:T(128)} %pad_add_fusion.1.ids, bf16[32,720,128]{2,1,0:T(8,128)(2,1)} %bitcast.15), custom_call_target="tpu_custom_call" | custom-call | flops 1 | bytes 1024 | tf_op jit(solution)/shard_map/pick/pallas_call | solution.py:88
  5.5 3.1 %collective-permute-start.5 = (bf16[5,720,128]{2,1,0:T(8,128)(2,1)}, bf16[5,720,128]{2,1,0:T(8,128)(2,1)S(1)}, u32[]{:S(2)}, u32[]{:S(2)}) collective-permute-start(bf16[5,720,128]{2,1,0:T(8,128)(2,1)} %pick.4), channel_id=1, source_target_pairs={{0,4},{4,8},{8,12},{12,0},{1,5},{5,9},{9,13},{13,1},{2,6},{6,10},{... | collective-permute-start | bytes 2764808 | tf_op jit(solution)/shard_map/ppermute | solution.py:331
  10.8 2.0 %broadcast_in_dim.35.pots = f32[6,2,360,128]{3,2,1,0:T(8,128)} broadcast(f32[6,2,360]{2,1,0:T(2,128)S(1)} %broadcast_in_dim.34), dimensions={0,1,2} | broadcast | bytes 2229120 | tf_op jit(solution)/shard_map/broadcast_in_dim | solution.py:322
  12.8 7.4 %couple.5 = (f32[5,6,128,128]{3,2,1,0:T(8,128)}, bf16[2,6,128,128]{3,2,1,0:T(8,128)(2,1)}, bf16[2,6,128,128]{3,2,1,0:T(8,128)(2,1)}, bf16[1,6,128,128]{3,2,1,0:T(8,128)(2,1)}) custom-call(s32[64]{0:T(128)} %plan.1, s32[3]{0:T(128)} %pad_add_fusion.1.ids, bf16[240,240]{1,0:T(8,128)(2,1)} %maximum_maximum_fusion.table, ...), custom_call_target="tpu_custom_call" | custom-call | flops 1 | bytes 1024 | tf_op jit(solution)/shard_map/couple/pallas_call | solution.py:177
  21.2 3.0 %pick.5 = bf16[5,720,128]{2,1,0:T(8,128)(2,1)} custom-call(s32[64]{0:T(128)} %plan.1, s32[3]{0:T(128)} %pad_add_fusion.1.ids, bf16[32,720,128]{2,1,0:T(8,128)(2,1)} %bitcast.18), custom_call_target="tpu_custom_call" | custom-call | flops 1 | bytes 1024 | tf_op jit(solution)/shard_map/pick/pallas_call | solution.py:88
  24.3 7.0 %collective-permute-done.5.other = bf16[5,720,128]{2,1,0:T(8,128)(2,1)S(1)} collective-permute-done((bf16[5,720,128]{2,1,0:T(8,128)(2,1)}, bf16[5,720,128]{2,1,0:T(8,128)(2,1)S(1)}, u32[]{:S(2)}, u32[]{:S(2)}) %collective-permute-start.5) | collective-permute-done | bytes 921632 | tf_op jit(solution)/shard_map/ppermute | solution.py:331
  31.3 1.7 %collective-permute-start.10 = (bf16[5,720,128]{2,1,0:T(8,128)(2,1)}, bf16[5,720,128]{2,1,0:T(8,128)(2,1)S(1)}, u32[]{:S(2)}, u32[]{:S(2)}) collective-permute-start(bf16[5,720,128]{2,1,0:T(8,128)(2,1)} %pick.5), channel_id=1, source_target_pairs={{0,12},{4,0},{8,4},{12,8},{1,13},{5,1},{9,5},{13,9},{2,14},{6,2},{... | collective-permute-start | bytes 2764808 | tf_op jit(solution)/shard_map/ppermute | solution.py:331
  33.1 1.2 add_convert_fusion.5
  34.2 0.8 pad_maximum_fusion
  35.1 1.5 %collective-permute-start.4 = (bf16[5,6,64,128]{3,2,1,0:T(8,128)(2,1)}, bf16[5,6,64,128]{3,2,1,0:T(8,128)(2,1)}, u32[]{:S(2)}, u32[]{:S(2)}) collective-permute-start(bf16[5,6,64,128]{3,2,1,0:T(8,128)(2,1)} %pad_maximum_fusion), channel_id=1, source_target_pairs={{0,2},{2,0},{1,3},{3,1},{4,6},{6,4},{5,7},{7,5},{8,10},{10,8},{9,1... | collective-permute-start | bytes 1474568 | tf_op jit(solution)/shard_map/ppermute | solution.py:351
  36.6 8.7 %couple.6 = (f32[5,6,128,128]{3,2,1,0:T(8,128)}, bf16[2,6,128,128]{3,2,1,0:T(8,128)(2,1)}, bf16[2,6,128,128]{3,2,1,0:T(8,128)(2,1)}, bf16[1,6,128,128]{3,2,1,0:T(8,128)(2,1)}) custom-call(s32[64]{0:T(128)} %plan.1, s32[3]{0:T(128)} %pad_add_fusion.1.ids, bf16[240,240]{1,0:T(8,128)(2,1)} %maximum_maximum_fusion.table, ...), custom_call_target="tpu_custom_call" | custom-call | flops 1 | bytes 1024 | tf_op jit(solution)/shard_map/couple/pallas_call | solution.py:177
  46.0 2.8 %pick.6 = bf16[3,720,128]{2,1,0:T(8,128)(2,1)} custom-call(s32[64]{0:T(128)} %plan.1, s32[3]{0:T(128)} %pad_add_fusion.1.ids, bf16[32,720,128]{2,1,0:T(8,128)(2,1)} %bitcast.20), custom_call_target="tpu_custom_call" | custom-call | flops 1 | bytes 1024 | tf_op jit(solution)/shard_map/pick/pallas_call | solution.py:88
  48.9 5.4 %collective-permute-done.10.other = bf16[5,720,128]{2,1,0:T(8,128)(2,1)S(1)} collective-permute-done((bf16[5,720,128]{2,1,0:T(8,128)(2,1)}, bf16[5,720,128]{2,1,0:T(8,128)(2,1)S(1)}, u32[]{:S(2)}, u32[]{:S(2)}) %collective-permute-start.10) | collective-permute-done | bytes 921632 | tf_op jit(solution)/shard_map/ppermute | solution.py:331
  54.3 0.9 copy-done.4
  55.2 8.7 %couple.7 = (f32[5,6,128,128]{3,2,1,0:T(8,128)}, bf16[2,6,128,128]{3,2,1,0:T(8,128)(2,1)}, bf16[2,6,128,128]{3,2,1,0:T(8,128)(2,1)}, bf16[1,6,128,128]{3,2,1,0:T(8,128)(2,1)}) custom-call(s32[64]{0:T(128)} %plan.1, s32[3]{0:T(128)} %pad_add_fusion.1.ids, bf16[240,240]{1,0:T(8,128)(2,1)} %maximum_maximum_fusion.table, ...), custom_call_target="tpu_custom_call" | custom-call | flops 1 | bytes 1024 | tf_op jit(solution)/shard_map/couple/pallas_call | solution.py:177
  64.6 1.1 add_convert_fusion.3
  65.8 1.6 %collective-permute-start.9 = (bf16[5,6,64,128]{3,2,1,0:T(8,128)(2,1)S(1)}, bf16[5,6,64,128]{3,2,1,0:T(8,128)(2,1)S(1)}, u32[]{:S(2)}, u32[]{:S(2)}) collective-permute-start(bf16[5,6,64,128]{3,2,1,0:T(8,128)(2,1)S(1)} %pad_maximum_fusion.1), channel_id=1, source_target_pairs={{0,2},{2,0},{1,3},{3,1},{4,6},{6,4},{5,7},{7,5},{8,10},{10,8},{9,1... | collective-permute-start | bytes 1474568 | tf_op jit(solution)/shard_map/ppermute | solution.py:351
  67.6 1.0 collective-permute-start.14
  68.6 2.4 %pick.7 = bf16[2,720,128]{2,1,0:T(8,128)(2,1)} custom-call(s32[64]{0:T(128)} %plan.1, s32[3]{0:T(128)} %pad_add_fusion.1.ids, bf16[32,720,128]{2,1,0:T(8,128)(2,1)} %bitcast.22), custom_call_target="tpu_custom_call" | custom-call | flops 1 | bytes 1024 | tf_op jit(solution)/shard_map/pick/pallas_call | solution.py:88
  71.6 8.3 %collective-permute-done.9.refs_9_ = bf16[5,6,64,128]{3,2,1,0:T(8,128)(2,1)S(1)} collective-permute-done((bf16[5,6,64,128]{3,2,1,0:T(8,128)(2,1)S(1)}, bf16[5,6,64,128]{3,2,1,0:T(8,128)(2,1)S(1)}, u32[]{:S(2)}, u32[]{:S(2)}) %collective-permute-start.9) | collective-permute-done | bytes 491552 | tf_op jit(solution)/shard_map/ppermute | solution.py:351
  80.7 3.8 %combine.2.refs_0_ = bf16[16,6,64,128]{3,2,1,0:T(8,128)(2,1)} custom-call(s32[64]{0:T(128)} %plan.1, f32[5,6,128,128]{3,2,1,0:T(8,128)} %get-tuple-element.44.refs_0_, bf16[2,6,128,128]{3,2,1,0:T(8,128)(2,1)} %collective-permute-done.1.refs_1_, bf16[2,6,128,128]{3,2,1,0:T(8,128)(2,1)} %collective-permute-done.2.refs_2_, bf16[1,6,128,128]{3,2,1,0:T(8,128)(2,1)} %copy-done.17, ...), custom_call_target="tpu_custom_call" | custom-call | flops 1 | bytes 1024 | tf_op jit(solution)/shard_map/combine/pallas_call | solution.py:248
  84.6 6.5 %couple.8 = (f32[3,6,128,128]{3,2,1,0:T(8,128)}, bf16[1,6,128,128]{3,2,1,0:T(8,128)(2,1)}, bf16[1,6,128,128]{3,2,1,0:T(8,128)(2,1)}, bf16[1,6,128,128]{3,2,1,0:T(8,128)(2,1)}) custom-call(s32[64]{0:T(128)} %plan.1, s32[3]{0:T(128)} %pad_add_fusion.1.ids, bf16[240,240]{1,0:T(8,128)(2,1)} %maximum_maximum_fusion.table, ...), custom_call_target="tpu_custom_call" | custom-call | flops 1 | bytes 1024 | tf_op jit(solution)/shard_map/couple/pallas_call | solution.py:177
  93.6 1.3 %add_convert_fusion.10 = (bf16[1,6,64,128]{3,2,1,0:T(8,128)(2,1)S(1)}, bf16[1,6,64,128]{3,2,1,0:T(8,128)(2,1)S(1)}, bf16[1,6,64,128]{3,2,1,0:T(8,128)(2,1)S(1)}) fusion(f32[3,6,128,128]{3,2,1,0:T(8,128)} %get-tuple-element.67.refs_6_, bf16[1,6,128,128]{3,2,1,0:T(8,128)(2,1)S(1)} %collective-permute-done.16.refs_7_, ...), kind=kLoop, calls=%fused_computation.15 | loop fusion | flops 442368 | bytes 1179648 | tf_op jit(solution)/shard_map/convert.2
  94.9 1.3 %collective-permute-start.20 = (bf16[3,6,64,128]{3,2,1,0:T(8,128)(2,1)S(1)}, bf16[3,6,64,128]{3,2,1,0:T(8,128)(2,1)S(1)}, u32[]{:S(2)}, u32[]{:S(2)}) collective-permute-start(bf16[3,6,64,128]{3,2,1,0:T(8,128)(2,1)S(1)} %pad_maximum_fusion.3), channel_id=1, source_target_pairs={{0,2},{2,0},{1,3},{3,1},{4,6},{6,4},{5,7},{7,5},{8,10},{10,8},{9,1... | collective-permute-start | bytes 884744 | tf_op jit(solution)/shard_map/ppermute | solution.py:351
  96.2 3.6 %couple.9 = (f32[2,6,128,128]{3,2,1,0:T(8,128)}, bf16[1,6,128,128]{3,2,1,0:T(8,128)(2,1)}, bf16[1,6,128,128]{3,2,1,0:T(8,128)(2,1)}) custom-call(s32[64]{0:T(128)} %plan.1, s32[3]{0:T(128)} %pad_add_fusion.1.ids, bf16[240,240]{1,0:T(8,128)(2,1)} %maximum_maximum_fusion.table, f32[6,2,360,128]{3,2,1,0:T(8,128)} %broadcast_in_dim.35.pots, ...), custom_call_target="tpu_custom_call" | custom-call | flops 1 | bytes 1024 | tf_op jit(solution)/shard_map/couple/pallas_call | solution.py:177
  100.0 4.1 %collective-permute-done.20.refs_10_ = bf16[3,6,64,128]{3,2,1,0:T(8,128)(2,1)S(1)} collective-permute-done((bf16[3,6,64,128]{3,2,1,0:T(8,128)(2,1)S(1)}, bf16[3,6,64,128]{3,2,1,0:T(8,128)(2,1)S(1)}, u32[]{:S(2)}, u32[]{:S(2)}) %collective-permute-start.20) | collective-permute-done | bytes 294944 | tf_op jit(solution)/shard_map/ppermute | solution.py:351
  104.0 1.6 %collective-permute-done.22.refs_13_ = bf16[1,6,128,128]{3,2,1,0:T(8,128)(2,1)S(1)} collective-permute-done((bf16[1,6,128,128]{3,2,1,0:T(8,128)(2,1)}, bf16[1,6,128,128]{3,2,1,0:T(8,128)(2,1)S(1)}, u32[]{:S(2)}, u32[]{:S(2)}) %collective-permute-start.22) | collective-permute-done | bytes 196640 | tf_op jit(solution)/shard_map/ppermute | solution.py:379
  105.7 1.1 add_convert_fusion.7
  106.8 1.4 %collective-permute-start.23 = (bf16[2,6,64,128]{3,2,1,0:T(8,128)(2,1)S(1)}, bf16[2,6,64,128]{3,2,1,0:T(8,128)(2,1)S(1)}, u32[]{:S(2)}, u32[]{:S(2)}) collective-permute-start(bf16[2,6,64,128]{3,2,1,0:T(8,128)(2,1)S(1)} %pad_maximum_fusion.4), channel_id=1, source_target_pairs={{0,2},{2,0},{1,3},{3,1},{4,6},{6,4},{5,7},{7,5},{8,10},{10,8},{9,1... | collective-permute-start | bytes 589832 | tf_op jit(solution)/shard_map/ppermute | solution.py:351
  108.2 5.7 %collective-permute-done.23.refs_14_ = bf16[2,6,64,128]{3,2,1,0:T(8,128)(2,1)S(1)} collective-permute-done((bf16[2,6,64,128]{3,2,1,0:T(8,128)(2,1)S(1)}, bf16[2,6,64,128]{3,2,1,0:T(8,128)(2,1)S(1)}, u32[]{:S(2)}, u32[]{:S(2)}) %collective-permute-start.23) | collective-permute-done | bytes 196640 | tf_op jit(solution)/shard_map/ppermute | solution.py:351
  114.6 3.8 %combine.3 = bf16[16,6,64,128]{3,2,1,0:T(8,128)(2,1)} custom-call(s32[64]{0:T(128)} %plan.1, bf16[16,6,64,128]{3,2,1,0:T(8,128)(2,1)} %combine.2.refs_0_, f32[5,6,128,128]{3,2,1,0:T(8,128)} %get-tuple-element.58.refs_1_, bf16[2,6,128,128]{3,2,1,0:T(8,128)(2,1)} %copy-done.5, bf16[2,6,128,128]{3,2,1,0:T(8,128)(2,1)} %copy-done.6, ...), custom_call_target="tpu_custom_call", output_to_operand_aliasing={{}: (1, {})} | custom-call | flops 1 | bytes 1024 | tf_op jit(solution)/shard_map/combine/pallas_call | solution.py:248
  (111 shorter events, 10.1 us)
Async XLA Ops:
  5.5 25.7 %collective-permute-start.5 = (bf16[5,720,128]{2,1,0:T(8,128)(2,1)}, bf16[5,720,128]{2,1,0:T(8,128)(2,1)S(1)}, u32[]{:S(2)}, u32[]{:S(2)}) collective-permute-start(bf16[5,720,128]{2,1,0:T(8,128)(2,1)} %pick.4), channel_id=1, source_target_pairs={{0,4},{4,8},{8,12},{12,0},{1,5},{5,9},{9,13},{13,1},{2,6},{6,10},{... | collective-permute-start | bytes 2764808 | tf_op jit(solution)/shard_map/ppermute | solution.py:331
  8.7 1.7 %collective-permute-start = (f32[3,3,240]{2,1,0:T(4,128)S(1)}, f32[3,3,240]{2,1,0:T(4,128)S(1)}, u32[]{:S(2)}, u32[]{:S(2)}) collective-permute-start(f32[3,3,240]{2,1,0:T(4,128)S(1)} %bitcast.29), channel_id=1, source_target_pairs={{0,1},{1,0},{2,3},{3,2},{4,5},{5,4},{6,7},{7,6},{8,9},{9,8},{10,11... | collective-permute-start | bytes 25928 | tf_op jit(solution)/shard_map/ppermute | solution.py:308
  20.2 12.8 %collective-permute-start.3 = (bf16[1,6,128,128]{3,2,1,0:T(8,128)(2,1)}, bf16[1,6,128,128]{3,2,1,0:T(8,128)(2,1)S(1)}, u32[]{:S(2)}, u32[]{:S(2)}) collective-permute-start(bf16[1,6,128,128]{3,2,1,0:T(8,128)(2,1)} %get-tuple-element.47), channel_id=1, source_target_pairs={{0,1},{1,0},{2,3},{3,2},{4,5},{5,4},{6,7},{7,6},{8,9},{9,8},{10,11... | collective-permute-start | bytes 589832 | tf_op jit(solution)/shard_map/ppermute | solution.py:379
  20.7 12.3 %collective-permute-start.1 = (bf16[2,6,128,128]{3,2,1,0:T(8,128)(2,1)}, bf16[2,6,128,128]{3,2,1,0:T(8,128)(2,1)}, u32[]{:S(2)}, u32[]{:S(2)}) collective-permute-start(bf16[2,6,128,128]{3,2,1,0:T(8,128)(2,1)} %get-tuple-element.45), channel_id=1, source_target_pairs={{0,1},{1,0},{2,3},{3,2},{4,5},{5,4},{6,7},{7,6},{8,9},{9,8},{10,11... | collective-permute-start | bytes 1179656 | tf_op jit(solution)/shard_map/ppermute | solution.py:379
  20.8 12.2 %copy-start.1 = (f32[5,6,128,128]{3,2,1,0:T(8,128)S(1)}, f32[5,6,128,128]{3,2,1,0:T(8,128)}, u32[]{:S(2)}) copy-start(f32[5,6,128,128]{3,2,1,0:T(8,128)} %get-tuple-element.44.refs_0_) | copy-start | bytes 5898244
  20.8 12.3 %collective-permute-start.2 = (bf16[2,6,128,128]{3,2,1,0:T(8,128)(2,1)}, bf16[2,6,128,128]{3,2,1,0:T(8,128)(2,1)}, u32[]{:S(2)}, u32[]{:S(2)}) collective-permute-start(bf16[2,6,128,128]{3,2,1,0:T(8,128)(2,1)} %get-tuple-element.46), channel_id=1, source_target_pairs={{0,1},{1,0},{2,3},{3,2},{4,5},{5,4},{6,7},{7,6},{8,9},{9,8},{10,11... | collective-permute-start | bytes 1179656 | tf_op jit(solution)/shard_map/ppermute | solution.py:379
  31.3 23.0 %collective-permute-start.10 = (bf16[5,720,128]{2,1,0:T(8,128)(2,1)}, bf16[5,720,128]{2,1,0:T(8,128)(2,1)S(1)}, u32[]{:S(2)}, u32[]{:S(2)}) collective-permute-start(bf16[5,720,128]{2,1,0:T(8,128)(2,1)} %pick.5), channel_id=1, source_target_pairs={{0,12},{4,0},{8,4},{12,8},{1,13},{5,1},{9,5},{13,9},{2,14},{6,2},{... | collective-permute-start | bytes 2764808 | tf_op jit(solution)/shard_map/ppermute | solution.py:331
  33.0 12.3 %copy-start.17 = (bf16[1,6,128,128]{3,2,1,0:T(8,128)(2,1)}, bf16[1,6,128,128]{3,2,1,0:T(8,128)(2,1)S(1)}, u32[]{:S(2)}) copy-start(bf16[1,6,128,128]{3,2,1,0:T(8,128)(2,1)S(1)} %collective-permute-done.3.refs_3_) | copy-start | bytes 589828
  35.1 19.2 %collective-permute-start.4 = (bf16[5,6,64,128]{3,2,1,0:T(8,128)(2,1)}, bf16[5,6,64,128]{3,2,1,0:T(8,128)(2,1)}, u32[]{:S(2)}, u32[]{:S(2)}) collective-permute-start(bf16[5,6,64,128]{3,2,1,0:T(8,128)(2,1)} %pad_maximum_fusion), channel_id=1, source_target_pairs={{0,2},{2,0},{1,3},{3,1},{4,6},{6,4},{5,7},{7,5},{8,10},{10,8},{9,1... | collective-permute-start | bytes 1474568 | tf_op jit(solution)/shard_map/ppermute | solution.py:351
  45.3 3.4 %collective-permute-start.8 = (bf16[1,6,128,128]{3,2,1,0:T(8,128)(2,1)}, bf16[1,6,128,128]{3,2,1,0:T(8,128)(2,1)S(1)}, u32[]{:S(2)}, u32[]{:S(2)}) collective-permute-start(bf16[1,6,128,128]{3,2,1,0:T(8,128)(2,1)} %get-tuple-element.53), channel_id=1, source_target_pairs={{0,1},{1,0},{2,3},{3,2},{4,5},{5,4},{6,7},{7,6},{8,9},{9,8},{10,11... | collective-permute-start | bytes 589832 | tf_op jit(solution)/shard_map/ppermute | solution.py:379
  45.4 8.9 %collective-permute-start.6 = (bf16[2,6,128,128]{3,2,1,0:T(8,128)(2,1)}, bf16[2,6,128,128]{3,2,1,0:T(8,128)(2,1)S(1)}, u32[]{:S(2)}, u32[]{:S(2)}) collective-permute-start(bf16[2,6,128,128]{3,2,1,0:T(8,128)(2,1)} %get-tuple-element.51), channel_id=1, source_target_pairs={{0,1},{1,0},{2,3},{3,2},{4,5},{5,4},{6,7},{7,6},{8,9},{9,8},{10,11... | collective-permute-start | bytes 1179656 | tf_op jit(solution)/shard_map/ppermute | solution.py:379
  45.9 8.4 %collective-permute-start.7 = (bf16[2,6,128,128]{3,2,1,0:T(8,128)(2,1)}, bf16[2,6,128,128]{3,2,1,0:T(8,128)(2,1)S(1)}, u32[]{:S(2)}, u32[]{:S(2)}) collective-permute-start(bf16[2,6,128,128]{3,2,1,0:T(8,128)(2,1)} %get-tuple-element.52), channel_id=1, source_target_pairs={{0,1},{1,0},{2,3},{3,2},{4,5},{5,4},{6,7},{7,6},{8,9},{9,8},{10,11... | collective-permute-start | bytes 1179656 | tf_op jit(solution)/shard_map/ppermute | solution.py:379
  48.8 15.2 %copy-start.18 = (bf16[1,6,128,128]{3,2,1,0:T(8,128)(2,1)}, bf16[1,6,128,128]{3,2,1,0:T(8,128)(2,1)S(1)}, u32[]{:S(2)}) copy-start(bf16[1,6,128,128]{3,2,1,0:T(8,128)(2,1)S(1)} %collective-permute-done.8.refs_8_) | copy-start | bytes 589828
  48.8 35.8 %collective-permute-start.15 = (bf16[3,720,128]{2,1,0:T(8,128)(2,1)}, bf16[3,720,128]{2,1,0:T(8,128)(2,1)}, u32[]{:S(2)}, u32[]{:S(2)}) collective-permute-start(bf16[3,720,128]{2,1,0:T(8,128)(2,1)} %pick.6), channel_id=1, source_target_pairs={{0,8},{4,12},{8,0},{12,4},{1,9},{5,13},{9,1},{13,5},{2,10},{6,14},... | collective-permute-start | bytes 1658888 | tf_op jit(solution)/shard_map/ppermute | solution.py:331
  54.3 9.6 %copy-start.7 = (bf16[2,6,128,128]{3,2,1,0:T(8,128)(2,1)}, bf16[2,6,128,128]{3,2,1,0:T(8,128)(2,1)S(1)}, u32[]{:S(2)}) copy-start(bf16[2,6,128,128]{3,2,1,0:T(8,128)(2,1)S(1)} %collective-permute-done.6.refs_6_) | copy-start | bytes 1179652
  54.3 9.7 %copy-start.8 = (bf16[2,6,128,128]{3,2,1,0:T(8,128)(2,1)}, bf16[2,6,128,128]{3,2,1,0:T(8,128)(2,1)S(1)}, u32[]{:S(2)}) copy-start(bf16[2,6,128,128]{3,2,1,0:T(8,128)(2,1)S(1)} %collective-permute-done.7.refs_7_) | copy-start | bytes 1179652
  63.9 3.5 %collective-permute-start.11 = (bf16[2,6,128,128]{3,2,1,0:T(8,128)(2,1)}, bf16[2,6,128,128]{3,2,1,0:T(8,128)(2,1)S(1)}, u32[]{:S(2)}, u32[]{:S(2)}) collective-permute-start(bf16[2,6,128,128]{3,2,1,0:T(8,128)(2,1)} %get-tuple-element.59), channel_id=1, source_target_pairs={{0,1},{1,0},{2,3},{3,2},{4,5},{5,4},{6,7},{7,6},{8,9},{9,8},{10,11... | collective-permute-start | bytes 1179656 | tf_op jit(solution)/shard_map/ppermute | solution.py:379
  64.0 3.4 %collective-permute-start.12 = (bf16[2,6,128,128]{3,2,1,0:T(8,128)(2,1)}, bf16[2,6,128,128]{3,2,1,0:T(8,128)(2,1)S(1)}, u32[]{:S(2)}, u32[]{:S(2)}) collective-permute-start(bf16[2,6,128,128]{3,2,1,0:T(8,128)(2,1)} %get-tuple-element.60), channel_id=1, source_target_pairs={{0,1},{1,0},{2,3},{3,2},{4,5},{5,4},{6,7},{7,6},{8,9},{9,8},{10,11... | collective-permute-start | bytes 1179656 | tf_op jit(solution)/shard_map/ppermute | solution.py:379
  64.5 2.9 %collective-permute-start.13 = (bf16[1,6,128,128]{3,2,1,0:T(8,128)(2,1)}, bf16[1,6,128,128]{3,2,1,0:T(8,128)(2,1)S(1)}, u32[]{:S(2)}, u32[]{:S(2)}) collective-permute-start(bf16[1,6,128,128]{3,2,1,0:T(8,128)(2,1)} %get-tuple-element.61), channel_id=1, source_target_pairs={{0,1},{1,0},{2,3},{3,2},{4,5},{5,4},{6,7},{7,6},{8,9},{9,8},{10,11... | collective-permute-start | bytes 589832 | tf_op jit(solution)/shard_map/ppermute | solution.py:379
  65.8 14.1 %collective-permute-start.9 = (bf16[5,6,64,128]{3,2,1,0:T(8,128)(2,1)S(1)}, bf16[5,6,64,128]{3,2,1,0:T(8,128)(2,1)S(1)}, u32[]{:S(2)}, u32[]{:S(2)}) collective-permute-start(bf16[5,6,64,128]{3,2,1,0:T(8,128)(2,1)S(1)} %pad_maximum_fusion.1), channel_id=1, source_target_pairs={{0,2},{2,0},{1,3},{3,1},{4,6},{6,4},{5,7},{7,5},{8,10},{10,8},{9,1... | collective-permute-start | bytes 1474568 | tf_op jit(solution)/shard_map/ppermute | solution.py:351
  67.6 24.0 %collective-permute-start.14 = (bf16[5,6,64,128]{3,2,1,0:T(8,128)(2,1)S(1)}, bf16[5,6,64,128]{3,2,1,0:T(8,128)(2,1)S(1)}, u32[]{:S(2)}, u32[]{:S(2)}) collective-permute-start(bf16[5,6,64,128]{3,2,1,0:T(8,128)(2,1)S(1)} %pad_maximum_fusion.2), channel_id=1, source_target_pairs={{0,2},{2,0},{1,3},{3,1},{4,6},{6,4},{5,7},{7,5},{8,10},{10,8},{9,1... | collective-permute-start | bytes 1474568 | tf_op jit(solution)/shard_map/ppermute | solution.py:351
  71.1 20.8 %collective-permute-start.18 = (bf16[2,720,128]{2,1,0:T(8,128)(2,1)}, bf16[2,720,128]{2,1,0:T(8,128)(2,1)S(1)}, u32[]{:S(2)}, u32[]{:S(2)}) collective-permute-start(bf16[2,720,128]{2,1,0:T(8,128)(2,1)} %pick.7), channel_id=1, source_target_pairs={{0,8},{4,12},{8,0},{12,4},{1,9},{5,13},{9,1},{13,5},{2,10},{6,14},... | collective-permute-start | bytes 1105928 | tf_op jit(solution)/shard_map/ppermute | solution.py:331
  91.1 1.7 %collective-permute-start.16 = (bf16[1,6,128,128]{3,2,1,0:T(8,128)(2,1)}, bf16[1,6,128,128]{3,2,1,0:T(8,128)(2,1)S(1)}, u32[]{:S(2)}, u32[]{:S(2)}) collective-permute-start(bf16[1,6,128,128]{3,2,1,0:T(8,128)(2,1)} %get-tuple-element.68), channel_id=1, source_target_pairs={{0,1},{1,0},{2,3},{3,2},{4,5},{5,4},{6,7},{7,6},{8,9},{9,8},{10,11... | collective-permute-start | bytes 589832 | tf_op jit(solution)/shard_map/ppermute | solution.py:379
  91.1 1.9 %collective-permute-start.17 = (bf16[1,6,128,128]{3,2,1,0:T(8,128)(2,1)}, bf16[1,6,128,128]{3,2,1,0:T(8,128)(2,1)S(1)}, u32[]{:S(2)}, u32[]{:S(2)}) collective-permute-start(bf16[1,6,128,128]{3,2,1,0:T(8,128)(2,1)} %get-tuple-element.69), channel_id=1, source_target_pairs={{0,1},{1,0},{2,3},{3,2},{4,5},{5,4},{6,7},{7,6},{8,9},{9,8},{10,11... | collective-permute-start | bytes 589832 | tf_op jit(solution)/shard_map/ppermute | solution.py:379
  91.6 8.3 %copy-start.9 = (bf16[5,6,64,128]{3,2,1,0:T(8,128)(2,1)}, bf16[5,6,64,128]{3,2,1,0:T(8,128)(2,1)S(1)}, u32[]{:S(2)}) copy-start(bf16[5,6,64,128]{3,2,1,0:T(8,128)(2,1)S(1)} %collective-permute-done.14.refs_5_) | copy-start | bytes 1474564
  91.9 1.7 %collective-permute-start.19 = (bf16[1,6,128,128]{3,2,1,0:T(8,128)(2,1)}, bf16[1,6,128,128]{3,2,1,0:T(8,128)(2,1)S(1)}, u32[]{:S(2)}, u32[]{:S(2)}) collective-permute-start(bf16[1,6,128,128]{3,2,1,0:T(8,128)(2,1)} %get-tuple-element.73), channel_id=1, source_target_pairs={{0,1},{1,0},{2,3},{3,2},{4,5},{5,4},{6,7},{7,6},{8,9},{9,8},{10,11... | collective-permute-start | bytes 589832 | tf_op jit(solution)/shard_map/ppermute | solution.py:379
  94.9 9.1 %collective-permute-start.20 = (bf16[3,6,64,128]{3,2,1,0:T(8,128)(2,1)S(1)}, bf16[3,6,64,128]{3,2,1,0:T(8,128)(2,1)S(1)}, u32[]{:S(2)}, u32[]{:S(2)}) collective-permute-start(bf16[3,6,64,128]{3,2,1,0:T(8,128)(2,1)S(1)} %pad_maximum_fusion.3), channel_id=1, source_target_pairs={{0,2},{2,0},{1,3},{3,1},{4,6},{6,4},{5,7},{7,5},{8,10},{10,8},{9,1... | collective-permute-start | bytes 884744 | tf_op jit(solution)/shard_map/ppermute | solution.py:351
  99.9 4.1 %collective-permute-start.21 = (bf16[1,6,128,128]{3,2,1,0:T(8,128)(2,1)}, bf16[1,6,128,128]{3,2,1,0:T(8,128)(2,1)S(1)}, u32[]{:S(2)}, u32[]{:S(2)}) collective-permute-start(bf16[1,6,128,128]{3,2,1,0:T(8,128)(2,1)} %get-tuple-element.78), channel_id=1, source_target_pairs={{0,1},{1,0},{2,3},{3,2},{4,5},{5,4},{6,7},{7,6},{8,9},{9,8},{10,11... | collective-permute-start | bytes 589832 | tf_op jit(solution)/shard_map/ppermute | solution.py:379
  104.0 9.8 %copy-start.20 = (bf16[3,6,64,128]{3,2,1,0:T(8,128)(2,1)}, bf16[3,6,64,128]{3,2,1,0:T(8,128)(2,1)S(1)}, u32[]{:S(2)}) copy-start(bf16[3,6,64,128]{3,2,1,0:T(8,128)(2,1)S(1)} %collective-permute-done.20.refs_10_) | copy-start | bytes 884740
  104.0 1.7 %collective-permute-start.22 = (bf16[1,6,128,128]{3,2,1,0:T(8,128)(2,1)}, bf16[1,6,128,128]{3,2,1,0:T(8,128)(2,1)S(1)}, u32[]{:S(2)}, u32[]{:S(2)}) collective-permute-start(bf16[1,6,128,128]{3,2,1,0:T(8,128)(2,1)} %get-tuple-element.80), channel_id=1, source_target_pairs={{0,1},{1,0},{2,3},{3,2},{4,5},{5,4},{6,7},{7,6},{8,9},{9,8},{10,11... | collective-permute-start | bytes 589832 | tf_op jit(solution)/shard_map/ppermute | solution.py:379
  104.0 9.8 %copy-start.14 = (bf16[1,6,128,128]{3,2,1,0:T(8,128)(2,1)}, bf16[1,6,128,128]{3,2,1,0:T(8,128)(2,1)S(1)}, u32[]{:S(2)}) copy-start(bf16[1,6,128,128]{3,2,1,0:T(8,128)(2,1)S(1)} %collective-permute-done.21.refs_12_) | copy-start | bytes 589828
  106.8 7.0 %collective-permute-start.23 = (bf16[2,6,64,128]{3,2,1,0:T(8,128)(2,1)S(1)}, bf16[2,6,64,128]{3,2,1,0:T(8,128)(2,1)S(1)}, u32[]{:S(2)}, u32[]{:S(2)}) collective-permute-start(bf16[2,6,64,128]{3,2,1,0:T(8,128)(2,1)S(1)} %pad_maximum_fusion.4), channel_id=1, source_target_pairs={{0,2},{2,0},{1,3},{3,1},{4,6},{6,4},{5,7},{7,5},{8,10},{10,8},{9,1... | collective-permute-start | bytes 589832 | tf_op jit(solution)/shard_map/ppermute | solution.py:351
  (16 other events, 70.6 us)
where the time goes:
time: 119 us; the launch traced here: 118 us
  Pallas kernels  55.7 us (47%)
  waiting for transfers between devices  34.1 us (29%)
  starting transfers between devices  15 us (13%)
  other arithmetic  8.13 us (7%)
  local copies, waits for them, and re-layouts  4.94 us (4%)
    pallas_call x5, Pallas kernels, couple(): pl.pallas_call(functools.partial(couple_kernel, shape), grid_spec=pltpu.P...  35 us
    ppermute x5, waiting for transfers between devices, exchange(): sent.append(lax.ppermute(total.astype(BF16), 'ga', pairs))  18.1 us
    ppermute x4, waiting for transfers between devices, body(): landed.append(lax.ppermute(give, 'pool', pairs))  12.7 us
    pallas_call x4, Pallas kernels, pick(): pl.pallas_call(functools.partial(pick_kernel, (2 * pools + shift) * cap +...  11.3 us
    pallas_call x2, Pallas kernels, combine(): pl.pallas_call(functools.partial(combine_kernel, shapes, others, scaling)...  7.63 us
    ppermute x5, starting transfers between devices, exchange(): sent.append(lax.ppermute(total.astype(BF16), 'ga', pairs))  6.68 us
    another operation x10, other arithmetic  5.42 us
    ppermute x4, starting transfers between devices, body(): landed.append(lax.ppermute(give, 'pool', pairs))  5.36 us
  transfers between devices with their start and end apart: 24, of which 10 were waited for; matrix products, arithmetic and copies ran while one was open for 6% of the time, Pallas kernels for 40%

commit v1 on v0

--- a/solution.py
+++ b/solution.py
@@ -379,6 +379,8 @@
         got.append([lax.ppermute(give, "pert", swap_cores) for give in gives_now])
     for i in range(len(terms), len(chunks)):
         exchange(i)
+    result = finish(last, result)
+    finished = last
     result = finish(len(chunks), result)
     return result.reshape(local_k, per_device, 2, share, bands)
 

time: 119 us -> 118 us (level)
  waiting for transfers between devices: 34.1 us -> 28.8 us
  Pallas kernels: 55.7 us -> 57.9 us
  starting transfers between devices: 15 us -> 16.5 us
    ppermute x5, waiting for transfers between devices: 18.1 us -> 12.3 us  [exchange(): sent.append(lax.ppermute(total.astype(BF16), 'ga', pairs))]
    pallas_call x2 -> x3, Pallas kernels: 7.63 us -> 9.84 us  [combine(): pl.pallas_call(functools.partial(combine_kernel, shapes, others, scaling)...]
  transfers between devices with their start and end apart: 24 -> 24, of which waited for: 10 -> 9; matrix products, arithmetic and copies ran while one was open for 6% -> 6% of each run, Pallas kernels for 40% -> 43%
where the time goes in v1:
time: 118 us; the launch traced here: 117 us
  Pallas kernels  57.9 us (49%)
  waiting for transfers between devices  28.8 us (24%)
  starting transfers between devices  16.5 us (14%)
  other arithmetic  8.13 us (7%)
  local copies, waits for them, and re-layouts  4.93 us (4%)
    pallas_call x5, Pallas kernels, couple(): pl.pallas_call(functools.partial(couple_kernel, shape), grid_spec=pltpu.P...  35 us
    ppermute x4, waiting for transfers between devices, body(): landed.append(lax.ppermute(give, 'pool', pairs))  13.2 us
    ppermute x5, waiting for transfers between devices, exchange(): sent.append(lax.ppermute(total.astype(BF16), 'ga', pairs))  12.3 us
    pallas_call x4, Pallas kernels, pick(): pl.pallas_call(functools.partial(pick_kernel, (2 * pools + shift) * cap +...  11.3 us
    pallas_call x3, Pallas kernels, combine(): pl.pallas_call(functools.partial(combine_kernel, shapes, others, scaling)...  9.84 us
    ppermute x5, starting transfers between devices, exchange(): sent.append(lax.ppermute(total.astype(BF16), 'ga', pairs))  7.13 us
    ppermute x4, starting transfers between devices, body(): landed.append(lax.ppermute(give, 'pool', pairs))  6.27 us
    another operation x10, other arithmetic  5.42 us
  transfers between devices with their start and end apart: 24, of which 9 were waited for; matrix products, arithmetic and copies ran while one was open for 6% of the time, Pallas kernels for 43%

profile of v1, /device:TPU:0, one launch (start us, length us, event | category | flops | bytes accessed | tf_op | source)
XLA Modules:
  0.0 116.8 jit_solution(9354828051852227831)
XLA Ops:
  0.7 1.8 %plan.1 = s32[64]{0:T(128)} custom-call(s32[3]{0:T(128)} %pad_add_fusion.1.ids, s32[64]{0:T(128)} %partners.1), custom_call_target="tpu_custom_call" | custom-call | flops 1 | bytes 1024 | tf_op jit(solution)/shard_map/plan/pallas_call | solution.py:65
  2.5 3.0 %pick.4 = bf16[5,720,128]{2,1,0:T(8,128)(2,1)} custom-call(s32[64]{0:T(128)} %plan.1, s32[3]{0:T(128)} %pad_add_fusion.1.ids, bf16[32,720,128]{2,1,0:T(8,128)(2,1)} %bitcast.15), custom_call_target="tpu_custom_call" | custom-call | flops 1 | bytes 1024 | tf_op jit(solution)/shard_map/pick/pallas_call | solution.py:88
  5.5 3.1 %collective-permute-start.5 = (bf16[5,720,128]{2,1,0:T(8,128)(2,1)}, bf16[5,720,128]{2,1,0:T(8,128)(2,1)S(1)}, u32[]{:S(2)}, u32[]{:S(2)}) collective-permute-start(bf16[5,720,128]{2,1,0:T(8,128)(2,1)} %pick.4), channel_id=1, source_target_pairs={{0,4},{4,8},{8,12},{12,0},{1,5},{5,9},{9,13},{13,1},{2,6},{6,10},{... | collective-permute-start | bytes 2764808 | tf_op jit(solution)/shard_map/ppermute | solution.py:331
  10.8 2.0 %broadcast_in_dim.35.pots = f32[6,2,360,128]{3,2,1,0:T(8,128)} broadcast(f32[6,2,360]{2,1,0:T(2,128)S(1)} %broadcast_in_dim.34), dimensions={0,1,2} | broadcast | bytes 2229120 | tf_op jit(solution)/shard_map/broadcast_in_dim | solution.py:322
  12.8 7.4 %couple.5 = (f32[5,6,128,128]{3,2,1,0:T(8,128)}, bf16[2,6,128,128]{3,2,1,0:T(8,128)(2,1)}, bf16[2,6,128,128]{3,2,1,0:T(8,128)(2,1)}, bf16[1,6,128,128]{3,2,1,0:T(8,128)(2,1)}) custom-call(s32[64]{0:T(128)} %plan.1, s32[3]{0:T(128)} %pad_add_fusion.1.ids, bf16[240,240]{1,0:T(8,128)(2,1)} %maximum_maximum_fusion.table, ...), custom_call_target="tpu_custom_call" | custom-call | flops 1 | bytes 1024 | tf_op jit(solution)/shard_map/couple/pallas_call | solution.py:177
  21.2 3.0 %pick.5 = bf16[5,720,128]{2,1,0:T(8,128)(2,1)} custom-call(s32[64]{0:T(128)} %plan.1, s32[3]{0:T(128)} %pad_add_fusion.1.ids, bf16[32,720,128]{2,1,0:T(8,128)(2,1)} %bitcast.18), custom_call_target="tpu_custom_call" | custom-call | flops 1 | bytes 1024 | tf_op jit(solution)/shard_map/pick/pallas_call | solution.py:88
  24.3 7.0 %collective-permute-done.5.other = bf16[5,720,128]{2,1,0:T(8,128)(2,1)S(1)} collective-permute-done((bf16[5,720,128]{2,1,0:T(8,128)(2,1)}, bf16[5,720,128]{2,1,0:T(8,128)(2,1)S(1)}, u32[]{:S(2)}, u32[]{:S(2)}) %collective-permute-start.5) | collective-permute-done | bytes 921632 | tf_op jit(solution)/shard_map/ppermute | solution.py:331
  31.3 1.7 %collective-permute-start.10 = (bf16[5,720,128]{2,1,0:T(8,128)(2,1)}, bf16[5,720,128]{2,1,0:T(8,128)(2,1)S(1)}, u32[]{:S(2)}, u32[]{:S(2)}) collective-permute-start(bf16[5,720,128]{2,1,0:T(8,128)(2,1)} %pick.5), channel_id=1, source_target_pairs={{0,12},{4,0},{8,4},{12,8},{1,13},{5,1},{9,5},{13,9},{2,14},{6,2},{... | collective-permute-start | bytes 2764808 | tf_op jit(solution)/shard_map/ppermute | solution.py:331
  33.1 1.2 add_convert_fusion.5
  35.1 1.5 %collective-permute-start.4 = (bf16[5,6,64,128]{3,2,1,0:T(8,128)(2,1)}, bf16[5,6,64,128]{3,2,1,0:T(8,128)(2,1)}, u32[]{:S(2)}, u32[]{:S(2)}) collective-permute-start(bf16[5,6,64,128]{3,2,1,0:T(8,128)(2,1)} %pad_maximum_fusion), channel_id=1, source_target_pairs={{0,2},{2,0},{1,3},{3,1},{4,6},{6,4},{5,7},{7,5},{8,10},{10,8},{9,1... | collective-permute-start | bytes 1474568 | tf_op jit(solution)/shard_map/ppermute | solution.py:351
  36.6 7.9 %couple.6 = (f32[5,6,128,128]{3,2,1,0:T(8,128)}, bf16[2,6,128,128]{3,2,1,0:T(8,128)(2,1)}, bf16[2,6,128,128]{3,2,1,0:T(8,128)(2,1)}, bf16[1,6,128,128]{3,2,1,0:T(8,128)(2,1)}) custom-call(s32[64]{0:T(128)} %plan.1, s32[3]{0:T(128)} %pad_add_fusion.1.ids, bf16[240,240]{1,0:T(8,128)(2,1)} %maximum_maximum_fusion.table, ...), custom_call_target="tpu_custom_call" | custom-call | flops 1 | bytes 1024 | tf_op jit(solution)/shard_map/couple/pallas_call | solution.py:177
  45.1 2.8 %pick.6 = bf16[3,720,128]{2,1,0:T(8,128)(2,1)} custom-call(s32[64]{0:T(128)} %plan.1, s32[3]{0:T(128)} %pad_add_fusion.1.ids, bf16[32,720,128]{2,1,0:T(8,128)(2,1)} %bitcast.20), custom_call_target="tpu_custom_call" | custom-call | flops 1 | bytes 1024 | tf_op jit(solution)/shard_map/pick/pallas_call | solution.py:88
  48.0 6.2 %collective-permute-done.10.other = bf16[5,720,128]{2,1,0:T(8,128)(2,1)S(1)} collective-permute-done((bf16[5,720,128]{2,1,0:T(8,128)(2,1)}, bf16[5,720,128]{2,1,0:T(8,128)(2,1)S(1)}, u32[]{:S(2)}, u32[]{:S(2)}) %collective-permute-start.10) | collective-permute-done | bytes 921632 | tf_op jit(solution)/shard_map/ppermute | solution.py:331
  55.2 8.7 %couple.7 = (f32[5,6,128,128]{3,2,1,0:T(8,128)}, bf16[2,6,128,128]{3,2,1,0:T(8,128)(2,1)}, bf16[2,6,128,128]{3,2,1,0:T(8,128)(2,1)}, bf16[1,6,128,128]{3,2,1,0:T(8,128)(2,1)}) custom-call(s32[64]{0:T(128)} %plan.1, s32[3]{0:T(128)} %pad_add_fusion.1.ids, bf16[240,240]{1,0:T(8,128)(2,1)} %maximum_maximum_fusion.table, ...), custom_call_target="tpu_custom_call" | custom-call | flops 1 | bytes 1024 | tf_op jit(solution)/shard_map/couple/pallas_call | solution.py:177
  64.6 1.1 add_convert_fusion.3
  65.8 1.6 %collective-permute-start.9 = (bf16[5,6,64,128]{3,2,1,0:T(8,128)(2,1)S(1)}, bf16[5,6,64,128]{3,2,1,0:T(8,128)(2,1)S(1)}, u32[]{:S(2)}, u32[]{:S(2)}) collective-permute-start(bf16[5,6,64,128]{3,2,1,0:T(8,128)(2,1)S(1)} %pad_maximum_fusion.1), channel_id=1, source_target_pairs={{0,2},{2,0},{1,3},{3,1},{4,6},{6,4},{5,7},{7,5},{8,10},{10,8},{9,1... | collective-permute-start | bytes 1474568 | tf_op jit(solution)/shard_map/ppermute | solution.py:351
  68.6 2.4 %pick.7 = bf16[2,720,128]{2,1,0:T(8,128)(2,1)} custom-call(s32[64]{0:T(128)} %plan.1, s32[3]{0:T(128)} %pad_add_fusion.1.ids, bf16[32,720,128]{2,1,0:T(8,128)(2,1)} %bitcast.22), custom_call_target="tpu_custom_call" | custom-call | flops 1 | bytes 1024 | tf_op jit(solution)/shard_map/pick/pallas_call | solution.py:88
  71.1 1.4 %collective-permute-start.18 = (bf16[2,720,128]{2,1,0:T(8,128)(2,1)}, bf16[2,720,128]{2,1,0:T(8,128)(2,1)S(1)}, u32[]{:S(2)}, u32[]{:S(2)}) collective-permute-start(bf16[2,720,128]{2,1,0:T(8,128)(2,1)} %pick.7), channel_id=1, source_target_pairs={{0,8},{4,12},{8,0},{12,4},{1,9},{5,13},{9,1},{13,5},{2,10},{6,14},... | collective-permute-start | bytes 1105928 | tf_op jit(solution)/shard_map/ppermute | solution.py:331
  72.5 7.4 %collective-permute-done.9.refs_9_ = bf16[5,6,64,128]{3,2,1,0:T(8,128)(2,1)S(1)} collective-permute-done((bf16[5,6,64,128]{3,2,1,0:T(8,128)(2,1)S(1)}, bf16[5,6,64,128]{3,2,1,0:T(8,128)(2,1)S(1)}, u32[]{:S(2)}, u32[]{:S(2)}) %collective-permute-start.9) | collective-permute-done | bytes 491552 | tf_op jit(solution)/shard_map/ppermute | solution.py:351
  80.7 3.8 %combine.3.refs_0_ = bf16[16,6,64,128]{3,2,1,0:T(8,128)(2,1)} custom-call(s32[64]{0:T(128)} %plan.1, f32[5,6,128,128]{3,2,1,0:T(8,128)} %get-tuple-element.44.refs_0_, bf16[2,6,128,128]{3,2,1,0:T(8,128)(2,1)} %collective-permute-done.1.refs_1_, bf16[2,6,128,128]{3,2,1,0:T(8,128)(2,1)} %collective-permute-done.2.refs_2_, bf16[1,6,128,128]{3,2,1,0:T(8,128)(2,1)} %copy-done.17, ...), custom_call_target="tpu_custom_call" | custom-call | flops 1 | bytes 1024 | tf_op jit(solution)/shard_map/combine/pallas_call | solution.py:248
  84.5 6.5 %couple.8 = (f32[3,6,128,128]{3,2,1,0:T(8,128)}, bf16[1,6,128,128]{3,2,1,0:T(8,128)(2,1)}, bf16[1,6,128,128]{3,2,1,0:T(8,128)(2,1)}, bf16[1,6,128,128]{3,2,1,0:T(8,128)(2,1)}) custom-call(s32[64]{0:T(128)} %plan.1, s32[3]{0:T(128)} %pad_add_fusion.1.ids, bf16[240,240]{1,0:T(8,128)(2,1)} %maximum_maximum_fusion.table, ...), custom_call_target="tpu_custom_call" | custom-call | flops 1 | bytes 1024 | tf_op jit(solution)/shard_map/couple/pallas_call | solution.py:177
  91.7 1.0 collective-permute-done.16.refs_7_
  93.3 1.3 %add_convert_fusion.10 = (bf16[1,6,64,128]{3,2,1,0:T(8,128)(2,1)S(1)}, bf16[1,6,64,128]{3,2,1,0:T(8,128)(2,1)S(1)}, bf16[1,6,64,128]{3,2,1,0:T(8,128)(2,1)S(1)}) fusion(f32[3,6,128,128]{3,2,1,0:T(8,128)} %get-tuple-element.67.refs_6_, bf16[1,6,128,128]{3,2,1,0:T(8,128)(2,1)S(1)} %collective-permute-done.16.refs_7_, ...), kind=kLoop, calls=%fused_computation.15 | loop fusion | flops 442368 | bytes 1179648 | tf_op jit(solution)/shard_map/convert.2
  94.6 1.6 %collective-permute-start.20 = (bf16[3,6,64,128]{3,2,1,0:T(8,128)(2,1)S(1)}, bf16[3,6,64,128]{3,2,1,0:T(8,128)(2,1)S(1)}, u32[]{:S(2)}, u32[]{:S(2)}) collective-permute-start(bf16[3,6,64,128]{3,2,1,0:T(8,128)(2,1)S(1)} %pad_maximum_fusion.3), channel_id=1, source_target_pairs={{0,2},{2,0},{1,3},{3,1},{4,6},{6,4},{5,7},{7,5},{8,10},{10,8},{9,1... | collective-permute-start | bytes 884744 | tf_op jit(solution)/shard_map/ppermute | solution.py:351
  96.2 4.5 %couple.9 = (f32[2,6,128,128]{3,2,1,0:T(8,128)}, bf16[1,6,128,128]{3,2,1,0:T(8,128)(2,1)}, bf16[1,6,128,128]{3,2,1,0:T(8,128)(2,1)}) custom-call(s32[64]{0:T(128)} %plan.1, s32[3]{0:T(128)} %pad_add_fusion.1.ids, bf16[240,240]{1,0:T(8,128)(2,1)} %maximum_maximum_fusion.table, f32[6,2,360,128]{3,2,1,0:T(8,128)} %broadcast_in_dim.35.pots, ...), custom_call_target="tpu_custom_call" | custom-call | flops 1 | bytes 1024 | tf_op jit(solution)/shard_map/couple/pallas_call | solution.py:177
  100.8 3.0 %collective-permute-done.20.refs_10_ = bf16[3,6,64,128]{3,2,1,0:T(8,128)(2,1)S(1)} collective-permute-done((bf16[3,6,64,128]{3,2,1,0:T(8,128)(2,1)S(1)}, bf16[3,6,64,128]{3,2,1,0:T(8,128)(2,1)S(1)}, u32[]{:S(2)}, u32[]{:S(2)}) %collective-permute-start.20) | collective-permute-done | bytes 294944 | tf_op jit(solution)/shard_map/ppermute | solution.py:351
  103.8 1.6 %collective-permute-done.22.refs_3_ = bf16[1,6,128,128]{3,2,1,0:T(8,128)(2,1)S(1)} collective-permute-done((bf16[1,6,128,128]{3,2,1,0:T(8,128)(2,1)}, bf16[1,6,128,128]{3,2,1,0:T(8,128)(2,1)S(1)}, u32[]{:S(2)}, u32[]{:S(2)}) %collective-permute-start.22) | collective-permute-done | bytes 196640 | tf_op jit(solution)/shard_map/ppermute | solution.py:379
  105.4 1.1 add_convert_fusion.7
  106.6 1.6 %collective-permute-start.23 = (bf16[2,6,64,128]{3,2,1,0:T(8,128)(2,1)S(1)}, bf16[2,6,64,128]{3,2,1,0:T(8,128)(2,1)S(1)}, u32[]{:S(2)}, u32[]{:S(2)}) collective-permute-start(bf16[2,6,64,128]{3,2,1,0:T(8,128)(2,1)S(1)} %pad_maximum_fusion.4), channel_id=1, source_target_pairs={{0,2},{2,0},{1,3},{3,1},{4,6},{6,4},{5,7},{7,5},{8,10},{10,8},{9,1... | collective-permute-start | bytes 589832 | tf_op jit(solution)/shard_map/ppermute | solution.py:351
  108.2 3.5 %combine.4.refs_0_ = bf16[16,6,64,128]{3,2,1,0:T(8,128)(2,1)} custom-call(s32[64]{0:T(128)} %plan.1, bf16[16,6,64,128]{3,2,1,0:T(8,128)(2,1)} %combine.3.refs_0_, f32[5,6,128,128]{3,2,1,0:T(8,128)} %get-tuple-element.58.refs_1_, bf16[2,6,128,128]{3,2,1,0:T(8,128)(2,1)} %copy-done.5, ...), custom_call_target="tpu_custom_call", output_to_operand_aliasing={{}: (1, {})} | custom-call | flops 1 | bytes 1024 | tf_op jit(solution)/shard_map/combine/pallas_call | solution.py:248
  111.7 1.9 %collective-permute-done.23.refs_4_ = bf16[2,6,64,128]{3,2,1,0:T(8,128)(2,1)S(1)} collective-permute-done((bf16[2,6,64,128]{3,2,1,0:T(8,128)(2,1)S(1)}, bf16[2,6,64,128]{3,2,1,0:T(8,128)(2,1)S(1)}, u32[]{:S(2)}, u32[]{:S(2)}) %collective-permute-start.23) | collective-permute-done | bytes 196640 | tf_op jit(solution)/shard_map/ppermute | solution.py:351
  114.3 2.5 %combine.5 = bf16[16,6,64,128]{3,2,1,0:T(8,128)(2,1)} custom-call(s32[64]{0:T(128)} %plan.1, bf16[16,6,64,128]{3,2,1,0:T(8,128)(2,1)} %combine.4.refs_0_, f32[2,6,128,128]{3,2,1,0:T(8,128)} %get-tuple-element.77.refs_1_, bf16[1,6,128,128]{3,2,1,0:T(8,128)(2,1)} %copy-done.11, bf16[1,6,128,128]{3,2,1,0:T(8,128)(2,1)} %copy-done.12, ...), custom_call_target="tpu_custom_call", output_to_operand_aliasing={{}: (1, {})} | custom-call | flops 1 | bytes 1024 | tf_op jit(solution)/shard_map/combine/pallas_call | solution.py:248
  (112 shorter events, 11.1 us)
Async XLA Ops:
  5.5 25.7 %collective-permute-start.5 = (bf16[5,720,128]{2,1,0:T(8,128)(2,1)}, bf16[5,720,128]{2,1,0:T(8,128)(2,1)S(1)}, u32[]{:S(2)}, u32[]{:S(2)}) collective-permute-start(bf16[5,720,128]{2,1,0:T(8,128)(2,1)} %pick.4), channel_id=1, source_target_pairs={{0,4},{4,8},{8,12},{12,0},{1,5},{5,9},{9,13},{13,1},{2,6},{6,10},{... | collective-permute-start | bytes 2764808 | tf_op jit(solution)/shard_map/ppermute | solution.py:331
  8.7 1.7 %collective-permute-start = (f32[3,3,240]{2,1,0:T(4,128)S(1)}, f32[3,3,240]{2,1,0:T(4,128)S(1)}, u32[]{:S(2)}, u32[]{:S(2)}) collective-permute-start(f32[3,3,240]{2,1,0:T(4,128)S(1)} %bitcast.29), channel_id=1, source_target_pairs={{0,1},{1,0},{2,3},{3,2},{4,5},{5,4},{6,7},{7,6},{8,9},{9,8},{10,11... | collective-permute-start | bytes 25928 | tf_op jit(solution)/shard_map/ppermute | solution.py:308
  20.2 12.8 %collective-permute-start.3 = (bf16[1,6,128,128]{3,2,1,0:T(8,128)(2,1)}, bf16[1,6,128,128]{3,2,1,0:T(8,128)(2,1)S(1)}, u32[]{:S(2)}, u32[]{:S(2)}) collective-permute-start(bf16[1,6,128,128]{3,2,1,0:T(8,128)(2,1)} %get-tuple-element.47), channel_id=1, source_target_pairs={{0,1},{1,0},{2,3},{3,2},{4,5},{5,4},{6,7},{7,6},{8,9},{9,8},{10,11... | collective-permute-start | bytes 589832 | tf_op jit(solution)/shard_map/ppermute | solution.py:379
  20.7 12.3 %collective-permute-start.1 = (bf16[2,6,128,128]{3,2,1,0:T(8,128)(2,1)}, bf16[2,6,128,128]{3,2,1,0:T(8,128)(2,1)}, u32[]{:S(2)}, u32[]{:S(2)}) collective-permute-start(bf16[2,6,128,128]{3,2,1,0:T(8,128)(2,1)} %get-tuple-element.45), channel_id=1, source_target_pairs={{0,1},{1,0},{2,3},{3,2},{4,5},{5,4},{6,7},{7,6},{8,9},{9,8},{10,11... | collective-permute-start | bytes 1179656 | tf_op jit(solution)/shard_map/ppermute | solution.py:379
  20.8 12.2 %copy-start.1 = (f32[5,6,128,128]{3,2,1,0:T(8,128)S(1)}, f32[5,6,128,128]{3,2,1,0:T(8,128)}, u32[]{:S(2)}) copy-start(f32[5,6,128,128]{3,2,1,0:T(8,128)} %get-tuple-element.44.refs_0_) | copy-start | bytes 5898244
  20.8 12.3 %collective-permute-start.2 = (bf16[2,6,128,128]{3,2,1,0:T(8,128)(2,1)}, bf16[2,6,128,128]{3,2,1,0:T(8,128)(2,1)}, u32[]{:S(2)}, u32[]{:S(2)}) collective-permute-start(bf16[2,6,128,128]{3,2,1,0:T(8,128)(2,1)} %get-tuple-element.46), channel_id=1, source_target_pairs={{0,1},{1,0},{2,3},{3,2},{4,5},{5,4},{6,7},{7,6},{8,9},{9,8},{10,11... | collective-permute-start | bytes 1179656 | tf_op jit(solution)/shard_map/ppermute | solution.py:379
  31.3 23.0 %collective-permute-start.10 = (bf16[5,720,128]{2,1,0:T(8,128)(2,1)}, bf16[5,720,128]{2,1,0:T(8,128)(2,1)S(1)}, u32[]{:S(2)}, u32[]{:S(2)}) collective-permute-start(bf16[5,720,128]{2,1,0:T(8,128)(2,1)} %pick.5), channel_id=1, source_target_pairs={{0,12},{4,0},{8,4},{12,8},{1,13},{5,1},{9,5},{13,9},{2,14},{6,2},{... | collective-permute-start | bytes 2764808 | tf_op jit(solution)/shard_map/ppermute | solution.py:331
  33.0 11.4 %copy-start.17 = (bf16[1,6,128,128]{3,2,1,0:T(8,128)(2,1)}, bf16[1,6,128,128]{3,2,1,0:T(8,128)(2,1)S(1)}, u32[]{:S(2)}) copy-start(bf16[1,6,128,128]{3,2,1,0:T(8,128)(2,1)S(1)} %collective-permute-done.3.refs_3_) | copy-start | bytes 589828
  35.1 19.2 %collective-permute-start.4 = (bf16[5,6,64,128]{3,2,1,0:T(8,128)(2,1)}, bf16[5,6,64,128]{3,2,1,0:T(8,128)(2,1)}, u32[]{:S(2)}, u32[]{:S(2)}) collective-permute-start(bf16[5,6,64,128]{3,2,1,0:T(8,128)(2,1)} %pad_maximum_fusion), channel_id=1, source_target_pairs={{0,2},{2,0},{1,3},{3,1},{4,6},{6,4},{5,7},{7,5},{8,10},{10,8},{9,1... | collective-permute-start | bytes 1474568 | tf_op jit(solution)/shard_map/ppermute | solution.py:351
  44.5 3.4 %collective-permute-start.8 = (bf16[1,6,128,128]{3,2,1,0:T(8,128)(2,1)}, bf16[1,6,128,128]{3,2,1,0:T(8,128)(2,1)S(1)}, u32[]{:S(2)}, u32[]{:S(2)}) collective-permute-start(bf16[1,6,128,128]{3,2,1,0:T(8,128)(2,1)} %get-tuple-element.53), channel_id=1, source_target_pairs={{0,1},{1,0},{2,3},{3,2},{4,5},{5,4},{6,7},{7,6},{8,9},{9,8},{10,11... | collective-permute-start | bytes 589832 | tf_op jit(solution)/shard_map/ppermute | solution.py:379
  44.5 9.7 %collective-permute-start.6 = (bf16[2,6,128,128]{3,2,1,0:T(8,128)(2,1)}, bf16[2,6,128,128]{3,2,1,0:T(8,128)(2,1)S(1)}, u32[]{:S(2)}, u32[]{:S(2)}) collective-permute-start(bf16[2,6,128,128]{3,2,1,0:T(8,128)(2,1)} %get-tuple-element.51), channel_id=1, source_target_pairs={{0,1},{1,0},{2,3},{3,2},{4,5},{5,4},{6,7},{7,6},{8,9},{9,8},{10,11... | collective-permute-start | bytes 1179656 | tf_op jit(solution)/shard_map/ppermute | solution.py:379
  45.0 9.2 %collective-permute-start.7 = (bf16[2,6,128,128]{3,2,1,0:T(8,128)(2,1)}, bf16[2,6,128,128]{3,2,1,0:T(8,128)(2,1)S(1)}, u32[]{:S(2)}, u32[]{:S(2)}) collective-permute-start(bf16[2,6,128,128]{3,2,1,0:T(8,128)(2,1)} %get-tuple-element.52), channel_id=1, source_target_pairs={{0,1},{1,0},{2,3},{3,2},{4,5},{5,4},{6,7},{7,6},{8,9},{9,8},{10,11... | collective-permute-start | bytes 1179656 | tf_op jit(solution)/shard_map/ppermute | solution.py:379
  47.9 16.0 %copy-start.18 = (bf16[1,6,128,128]{3,2,1,0:T(8,128)(2,1)}, bf16[1,6,128,128]{3,2,1,0:T(8,128)(2,1)S(1)}, u32[]{:S(2)}) copy-start(bf16[1,6,128,128]{3,2,1,0:T(8,128)(2,1)S(1)} %collective-permute-done.8.refs_8_) | copy-start | bytes 589828
  47.9 36.6 %collective-permute-start.15 = (bf16[3,720,128]{2,1,0:T(8,128)(2,1)}, bf16[3,720,128]{2,1,0:T(8,128)(2,1)}, u32[]{:S(2)}, u32[]{:S(2)}) collective-permute-start(bf16[3,720,128]{2,1,0:T(8,128)(2,1)} %pick.6), channel_id=1, source_target_pairs={{0,8},{4,12},{8,0},{12,4},{1,9},{5,13},{9,1},{13,5},{2,10},{6,14},... | collective-permute-start | bytes 1658888 | tf_op jit(solution)/shard_map/ppermute | solution.py:331
  54.3 9.6 %copy-start.7 = (bf16[2,6,128,128]{3,2,1,0:T(8,128)(2,1)}, bf16[2,6,128,128]{3,2,1,0:T(8,128)(2,1)S(1)}, u32[]{:S(2)}) copy-start(bf16[2,6,128,128]{3,2,1,0:T(8,128)(2,1)S(1)} %collective-permute-done.6.refs_6_) | copy-start | bytes 1179652
  54.3 9.7 %copy-start.8 = (bf16[2,6,128,128]{3,2,1,0:T(8,128)(2,1)}, bf16[2,6,128,128]{3,2,1,0:T(8,128)(2,1)S(1)}, u32[]{:S(2)}) copy-start(bf16[2,6,128,128]{3,2,1,0:T(8,128)(2,1)S(1)} %collective-permute-done.7.refs_7_) | copy-start | bytes 1179652
  63.9 3.5 %collective-permute-start.11 = (bf16[2,6,128,128]{3,2,1,0:T(8,128)(2,1)}, bf16[2,6,128,128]{3,2,1,0:T(8,128)(2,1)S(1)}, u32[]{:S(2)}, u32[]{:S(2)}) collective-permute-start(bf16[2,6,128,128]{3,2,1,0:T(8,128)(2,1)} %get-tuple-element.59), channel_id=1, source_target_pairs={{0,1},{1,0},{2,3},{3,2},{4,5},{5,4},{6,7},{7,6},{8,9},{9,8},{10,11... | collective-permute-start | bytes 1179656 | tf_op jit(solution)/shard_map/ppermute | solution.py:379
  64.0 3.4 %collective-permute-start.12 = (bf16[2,6,128,128]{3,2,1,0:T(8,128)(2,1)}, bf16[2,6,128,128]{3,2,1,0:T(8,128)(2,1)S(1)}, u32[]{:S(2)}, u32[]{:S(2)}) collective-permute-start(bf16[2,6,128,128]{3,2,1,0:T(8,128)(2,1)} %get-tuple-element.60), channel_id=1, source_target_pairs={{0,1},{1,0},{2,3},{3,2},{4,5},{5,4},{6,7},{7,6},{8,9},{9,8},{10,11... | collective-permute-start | bytes 1179656 | tf_op jit(solution)/shard_map/ppermute | solution.py:379
  64.5 2.9 %collective-permute-start.13 = (bf16[1,6,128,128]{3,2,1,0:T(8,128)(2,1)}, bf16[1,6,128,128]{3,2,1,0:T(8,128)(2,1)S(1)}, u32[]{:S(2)}, u32[]{:S(2)}) collective-permute-start(bf16[1,6,128,128]{3,2,1,0:T(8,128)(2,1)} %get-tuple-element.61), channel_id=1, source_target_pairs={{0,1},{1,0},{2,3},{3,2},{4,5},{5,4},{6,7},{7,6},{8,9},{9,8},{10,11... | collective-permute-start | bytes 589832 | tf_op jit(solution)/shard_map/ppermute | solution.py:379
  65.8 14.1 %collective-permute-start.9 = (bf16[5,6,64,128]{3,2,1,0:T(8,128)(2,1)S(1)}, bf16[5,6,64,128]{3,2,1,0:T(8,128)(2,1)S(1)}, u32[]{:S(2)}, u32[]{:S(2)}) collective-permute-start(bf16[5,6,64,128]{3,2,1,0:T(8,128)(2,1)S(1)} %pad_maximum_fusion.1), channel_id=1, source_target_pairs={{0,2},{2,0},{1,3},{3,1},{4,6},{6,4},{5,7},{7,5},{8,10},{10,8},{9,1... | collective-permute-start | bytes 1474568 | tf_op jit(solution)/shard_map/ppermute | solution.py:351
  67.6 23.9 %collective-permute-start.14 = (bf16[5,6,64,128]{3,2,1,0:T(8,128)(2,1)S(1)}, bf16[5,6,64,128]{3,2,1,0:T(8,128)(2,1)S(1)}, u32[]{:S(2)}, u32[]{:S(2)}) collective-permute-start(bf16[5,6,64,128]{3,2,1,0:T(8,128)(2,1)S(1)} %pad_maximum_fusion.2), channel_id=1, source_target_pairs={{0,2},{2,0},{1,3},{3,1},{4,6},{6,4},{5,7},{7,5},{8,10},{10,8},{9,1... | collective-permute-start | bytes 1474568 | tf_op jit(solution)/shard_map/ppermute | solution.py:351
  71.1 20.5 %collective-permute-start.18 = (bf16[2,720,128]{2,1,0:T(8,128)(2,1)}, bf16[2,720,128]{2,1,0:T(8,128)(2,1)S(1)}, u32[]{:S(2)}, u32[]{:S(2)}) collective-permute-start(bf16[2,720,128]{2,1,0:T(8,128)(2,1)} %pick.7), channel_id=1, source_target_pairs={{0,8},{4,12},{8,0},{12,4},{1,9},{5,13},{9,1},{13,5},{2,10},{6,14},... | collective-permute-start | bytes 1105928 | tf_op jit(solution)/shard_map/ppermute | solution.py:331
  91.0 1.7 %collective-permute-start.16 = (bf16[1,6,128,128]{3,2,1,0:T(8,128)(2,1)}, bf16[1,6,128,128]{3,2,1,0:T(8,128)(2,1)S(1)}, u32[]{:S(2)}, u32[]{:S(2)}) collective-permute-start(bf16[1,6,128,128]{3,2,1,0:T(8,128)(2,1)} %get-tuple-element.68), channel_id=1, source_target_pairs={{0,1},{1,0},{2,3},{3,2},{4,5},{5,4},{6,7},{7,6},{8,9},{9,8},{10,11... | collective-permute-start | bytes 589832 | tf_op jit(solution)/shard_map/ppermute | solution.py:379
  91.0 1.9 %collective-permute-start.17 = (bf16[1,6,128,128]{3,2,1,0:T(8,128)(2,1)}, bf16[1,6,128,128]{3,2,1,0:T(8,128)(2,1)S(1)}, u32[]{:S(2)}, u32[]{:S(2)}) collective-permute-start(bf16[1,6,128,128]{3,2,1,0:T(8,128)(2,1)} %get-tuple-element.69), channel_id=1, source_target_pairs={{0,1},{1,0},{2,3},{3,2},{4,5},{5,4},{6,7},{7,6},{8,9},{9,8},{10,11... | collective-permute-start | bytes 589832 | tf_op jit(solution)/shard_map/ppermute | solution.py:379
  91.5 9.1 %copy-start.9 = (bf16[5,6,64,128]{3,2,1,0:T(8,128)(2,1)}, bf16[5,6,64,128]{3,2,1,0:T(8,128)(2,1)S(1)}, u32[]{:S(2)}) copy-start(bf16[5,6,64,128]{3,2,1,0:T(8,128)(2,1)S(1)} %collective-permute-done.14.refs_5_) | copy-start | bytes 1474564
  91.6 1.7 %collective-permute-start.19 = (bf16[1,6,128,128]{3,2,1,0:T(8,128)(2,1)}, bf16[1,6,128,128]{3,2,1,0:T(8,128)(2,1)S(1)}, u32[]{:S(2)}, u32[]{:S(2)}) collective-permute-start(bf16[1,6,128,128]{3,2,1,0:T(8,128)(2,1)} %get-tuple-element.73), channel_id=1, source_target_pairs={{0,1},{1,0},{2,3},{3,2},{4,5},{5,4},{6,7},{7,6},{8,9},{9,8},{10,11... | collective-permute-start | bytes 589832 | tf_op jit(solution)/shard_map/ppermute | solution.py:379
  92.7 8.0 %copy-start.13 = (bf16[1,6,128,128]{3,2,1,0:T(8,128)(2,1)}, bf16[1,6,128,128]{3,2,1,0:T(8,128)(2,1)S(1)}, u32[]{:S(2)}) copy-start(bf16[1,6,128,128]{3,2,1,0:T(8,128)(2,1)S(1)} %collective-permute-done.16.refs_7_) | copy-start | bytes 589828
  94.6 9.2 %collective-permute-start.20 = (bf16[3,6,64,128]{3,2,1,0:T(8,128)(2,1)S(1)}, bf16[3,6,64,128]{3,2,1,0:T(8,128)(2,1)S(1)}, u32[]{:S(2)}, u32[]{:S(2)}) collective-permute-start(bf16[3,6,64,128]{3,2,1,0:T(8,128)(2,1)S(1)} %pad_maximum_fusion.3), channel_id=1, source_target_pairs={{0,2},{2,0},{1,3},{3,1},{4,6},{6,4},{5,7},{7,5},{8,10},{10,8},{9,1... | collective-permute-start | bytes 884744 | tf_op jit(solution)/shard_map/ppermute | solution.py:351
  100.7 3.1 %collective-permute-start.21 = (bf16[1,6,128,128]{3,2,1,0:T(8,128)(2,1)}, bf16[1,6,128,128]{3,2,1,0:T(8,128)(2,1)S(1)}, u32[]{:S(2)}, u32[]{:S(2)}) collective-permute-start(bf16[1,6,128,128]{3,2,1,0:T(8,128)(2,1)} %get-tuple-element.78), channel_id=1, source_target_pairs={{0,1},{1,0},{2,3},{3,2},{4,5},{5,4},{6,7},{7,6},{8,9},{9,8},{10,11... | collective-permute-start | bytes 589832 | tf_op jit(solution)/shard_map/ppermute | solution.py:379
  103.8 1.7 %collective-permute-start.22 = (bf16[1,6,128,128]{3,2,1,0:T(8,128)(2,1)}, bf16[1,6,128,128]{3,2,1,0:T(8,128)(2,1)S(1)}, u32[]{:S(2)}, u32[]{:S(2)}) collective-permute-start(bf16[1,6,128,128]{3,2,1,0:T(8,128)(2,1)} %get-tuple-element.80), channel_id=1, source_target_pairs={{0,1},{1,0},{2,3},{3,2},{4,5},{5,4},{6,7},{7,6},{8,9},{9,8},{10,11... | collective-permute-start | bytes 589832 | tf_op jit(solution)/shard_map/ppermute | solution.py:379
  103.8 7.9 %copy-start.11 = (bf16[1,6,128,128]{3,2,1,0:T(8,128)(2,1)}, bf16[1,6,128,128]{3,2,1,0:T(8,128)(2,1)S(1)}, u32[]{:S(2)}) copy-start(bf16[1,6,128,128]{3,2,1,0:T(8,128)(2,1)S(1)} %collective-permute-done.21.refs_2_) | copy-start | bytes 589828
  106.6 7.0 %collective-permute-start.23 = (bf16[2,6,64,128]{3,2,1,0:T(8,128)(2,1)S(1)}, bf16[2,6,64,128]{3,2,1,0:T(8,128)(2,1)S(1)}, u32[]{:S(2)}, u32[]{:S(2)}) collective-permute-start(bf16[2,6,64,128]{3,2,1,0:T(8,128)(2,1)S(1)} %pad_maximum_fusion.4), channel_id=1, source_target_pairs={{0,2},{2,0},{1,3},{3,1},{4,6},{6,4},{5,7},{7,5},{8,10},{10,8},{9,1... | collective-permute-start | bytes 589832 | tf_op jit(solution)/shard_map/ppermute | solution.py:351
  (16 other events, 68.2 us)

commit v2 on v1

--- a/solution.py
+++ b/solution.py
@@ -370,6 +370,8 @@
             result = finish(i - LAG_GROUP + 1, result)
             finished = i - LAG_GROUP + 1
             other = after(other, result)
+        if i == 0:
+            other = after(other, *gives[2:3])
         keep, *gives_now = couple(plan, ids, table, pots, waves, other, chunk, pools, cap, groups)
         kept.append(keep)
         if i >= last - 1:

time: 118 us -> 127 us (1.076)
  the two profiles are of different devices: /device:TPU:0 before, /device:TPU:14 now
where the time goes in v2:
time: 127 us; the launch traced here: 126 us
  Pallas kernels  57.8 us (46%)
  waiting for transfers between devices  42.3 us (33%)
  starting transfers between devices  10.3 us (8%)
  other arithmetic  9.12 us (7%)
  local copies, waits for them, and re-layouts  5.69 us (4%)
    pallas_call x5, Pallas kernels, couple(): pl.pallas_call(functools.partial(couple_kernel, shape), grid_spec=pltpu.P...  35 us
    ppermute x4, waiting for transfers between devices, body(): landed.append(lax.ppermute(give, 'pool', pairs))  20.7 us
    ppermute x5, waiting for transfers between devices, exchange(): sent.append(lax.ppermute(total.astype(BF16), 'ga', pairs))  16.5 us
    pallas_call x4, Pallas kernels, pick(): pl.pallas_call(functools.partial(pick_kernel, (2 * pools + shift) * cap +...  11.2 us
    pallas_call x3, Pallas kernels, combine(): pl.pallas_call(functools.partial(combine_kernel, shapes, others, scaling)...  9.84 us
    another operation x10, other arithmetic  6.44 us
    ppermute x14, waiting for transfers between devices, body(): got.append([lax.ppermute(give, 'pert', swap_cores) for give in gives_now])  5.1 us
    ppermute x4, starting transfers between devices, body(): landed.append(lax.ppermute(give, 'pool', pairs))  4.74 us
  transfers between devices with their start and end apart: 24, of which 11 were waited for; matrix products, arithmetic and copies ran while one was open for 7% of the time, Pallas kernels for 40%

profile of v2, /device:TPU:14, one launch (start us, length us, event | category | flops | bytes accessed | tf_op | source)
XLA Modules:
  0.0 125.8 jit_solution(3456504557861978262)
XLA Ops:
  0.6 1.8 %plan.1 = s32[64]{0:T(128)} custom-call(s32[3]{0:T(128)} %pad_add_fusion.1.ids, s32[64]{0:T(128)} %partners.1), custom_call_target="tpu_custom_call" | custom-call | flops 1 | bytes 1024 | tf_op jit(solution)/shard_map/plan/pallas_call | solution.py:65
  2.5 3.0 %pick.4 = bf16[5,720,128]{2,1,0:T(8,128)(2,1)} custom-call(s32[64]{0:T(128)} %plan.1, s32[3]{0:T(128)} %pad_add_fusion.1.ids, bf16[32,720,128]{2,1,0:T(8,128)(2,1)} %bitcast.15), custom_call_target="tpu_custom_call" | custom-call | flops 1 | bytes 1024 | tf_op jit(solution)/shard_map/pick/pallas_call | solution.py:88
  5.5 1.6 %collective-permute-start.5 = (bf16[5,720,128]{2,1,0:T(8,128)(2,1)}, bf16[5,720,128]{2,1,0:T(8,128)(2,1)S(1)}, u32[]{:S(2)}, u32[]{:S(2)}) collective-permute-start(bf16[5,720,128]{2,1,0:T(8,128)(2,1)} %pick.4), channel_id=1, source_target_pairs={{0,4},{4,8},{8,12},{12,0},{1,5},{5,9},{9,13},{13,1},{2,6},{6,10},{... | collective-permute-start | bytes 2764808 | tf_op jit(solution)/shard_map/ppermute | solution.py:331
  8.8 2.7 %pick.5 = bf16[3,720,128]{2,1,0:T(8,128)(2,1)} custom-call(s32[64]{0:T(128)} %plan.1, s32[3]{0:T(128)} %pad_add_fusion.1.ids, bf16[32,720,128]{2,1,0:T(8,128)(2,1)} %bitcast.16), custom_call_target="tpu_custom_call" | custom-call | flops 1 | bytes 1024 | tf_op jit(solution)/shard_map/pick/pallas_call | solution.py:88
  12.0 2.0 %broadcast_in_dim.35.pots = f32[6,2,360,128]{3,2,1,0:T(8,128)} broadcast(f32[6,2,360]{2,1,0:T(2,128)S(1)} %broadcast_in_dim.34), dimensions={0,1,2} | broadcast | bytes 2229120 | tf_op jit(solution)/shard_map/broadcast_in_dim | solution.py:322
  14.0 7.4 %couple.5 = (f32[5,6,128,128]{3,2,1,0:T(8,128)}, bf16[2,6,128,128]{3,2,1,0:T(8,128)(2,1)}, bf16[2,6,128,128]{3,2,1,0:T(8,128)(2,1)}, bf16[1,6,128,128]{3,2,1,0:T(8,128)(2,1)}) custom-call(s32[64]{0:T(128)} %plan.1, s32[3]{0:T(128)} %pad_add_fusion.1.ids, bf16[240,240]{1,0:T(8,128)(2,1)} %maximum_maximum_fusion.table, ...), custom_call_target="tpu_custom_call" | custom-call | flops 1 | bytes 1024 | tf_op jit(solution)/shard_map/couple/pallas_call | solution.py:177
  22.4 3.0 %pick.6 = bf16[5,720,128]{2,1,0:T(8,128)(2,1)} custom-call(s32[64]{0:T(128)} %plan.1, s32[3]{0:T(128)} %pad_add_fusion.1.ids, bf16[32,720,128]{2,1,0:T(8,128)(2,1)} %bitcast.19), custom_call_target="tpu_custom_call" | custom-call | flops 1 | bytes 1024 | tf_op jit(solution)/shard_map/pick/pallas_call | solution.py:88
  25.5 2.4 %collective-permute-done.5.other = bf16[5,720,128]{2,1,0:T(8,128)(2,1)S(1)} collective-permute-done((bf16[5,720,128]{2,1,0:T(8,128)(2,1)}, bf16[5,720,128]{2,1,0:T(8,128)(2,1)S(1)}, u32[]{:S(2)}, u32[]{:S(2)}) %collective-permute-start.5) | collective-permute-done | bytes 921632 | tf_op jit(solution)/shard_map/ppermute | solution.py:331
  27.9 2.3 %collective-permute-start.10 = (bf16[5,720,128]{2,1,0:T(8,128)(2,1)}, bf16[5,720,128]{2,1,0:T(8,128)(2,1)S(1)}, u32[]{:S(2)}, u32[]{:S(2)}) collective-permute-start(bf16[5,720,128]{2,1,0:T(8,128)(2,1)} %pick.6), channel_id=1, source_target_pairs={{0,12},{4,0},{8,4},{12,8},{1,13},{5,1},{9,5},{13,9},{2,14},{6,2},{... | collective-permute-start | bytes 2764808 | tf_op jit(solution)/shard_map/ppermute | solution.py:331
  30.3 1.2 add_convert_fusion.5
  31.5 0.8 pad_maximum_fusion
  32.9 8.7 %couple.6 = (f32[5,6,128,128]{3,2,1,0:T(8,128)}, bf16[2,6,128,128]{3,2,1,0:T(8,128)(2,1)}, bf16[2,6,128,128]{3,2,1,0:T(8,128)(2,1)}, bf16[1,6,128,128]{3,2,1,0:T(8,128)(2,1)}) custom-call(s32[64]{0:T(128)} %plan.1, s32[3]{0:T(128)} %pad_add_fusion.1.ids, bf16[240,240]{1,0:T(8,128)(2,1)} %maximum_maximum_fusion.table, ...), custom_call_target="tpu_custom_call" | custom-call | flops 1 | bytes 1024 | tf_op jit(solution)/shard_map/couple/pallas_call | solution.py:177
  42.2 1.1 collective-permute-done.8.refs_8_
  44.0 1.0 add_convert_fusion.12
  45.0 18.3 %collective-permute-done.10.other = bf16[5,720,128]{2,1,0:T(8,128)(2,1)S(1)} collective-permute-done((bf16[5,720,128]{2,1,0:T(8,128)(2,1)}, bf16[5,720,128]{2,1,0:T(8,128)(2,1)S(1)}, u32[]{:S(2)}, u32[]{:S(2)}) %collective-permute-start.10) | collective-permute-done | bytes 921632 | tf_op jit(solution)/shard_map/ppermute | solution.py:331
  63.3 0.9 copy-done.3
  64.2 7.8 %couple.7 = (f32[5,6,128,128]{3,2,1,0:T(8,128)}, bf16[2,6,128,128]{3,2,1,0:T(8,128)(2,1)}, bf16[2,6,128,128]{3,2,1,0:T(8,128)(2,1)}, bf16[1,6,128,128]{3,2,1,0:T(8,128)(2,1)}) custom-call(s32[64]{0:T(128)} %plan.1, s32[3]{0:T(128)} %pad_add_fusion.1.ids, bf16[240,240]{1,0:T(8,128)(2,1)} %maximum_maximum_fusion.table, ...), custom_call_target="tpu_custom_call" | custom-call | flops 1 | bytes 1024 | tf_op jit(solution)/shard_map/couple/pallas_call | solution.py:177
  72.7 1.2 add_convert_fusion.3
  75.2 1.3 %collective-permute-start.14 = (bf16[5,6,64,128]{3,2,1,0:T(8,128)(2,1)S(1)}, bf16[5,6,64,128]{3,2,1,0:T(8,128)(2,1)S(1)}, u32[]{:S(2)}, u32[]{:S(2)}) collective-permute-start(bf16[5,6,64,128]{3,2,1,0:T(8,128)(2,1)S(1)} %pad_maximum_fusion.2), channel_id=1, source_target_pairs={{0,2},{2,0},{1,3},{3,1},{4,6},{6,4},{5,7},{7,5},{8,10},{10,8},{9,1... | collective-permute-start | bytes 1474568 | tf_op jit(solution)/shard_map/ppermute | solution.py:351
  76.4 2.5 %pick.7 = bf16[2,720,128]{2,1,0:T(8,128)(2,1)} custom-call(s32[64]{0:T(128)} %plan.1, s32[3]{0:T(128)} %pad_add_fusion.1.ids, bf16[32,720,128]{2,1,0:T(8,128)(2,1)} %bitcast.22), custom_call_target="tpu_custom_call" | custom-call | flops 1 | bytes 1024 | tf_op jit(solution)/shard_map/pick/pallas_call | solution.py:88
  79.0 9.1 %collective-permute-done.9.refs_9_ = bf16[5,6,64,128]{3,2,1,0:T(8,128)(2,1)S(1)} collective-permute-done((bf16[5,6,64,128]{3,2,1,0:T(8,128)(2,1)S(1)}, bf16[5,6,64,128]{3,2,1,0:T(8,128)(2,1)S(1)}, u32[]{:S(2)}, u32[]{:S(2)}) %collective-permute-start.9) | collective-permute-done | bytes 491552 | tf_op jit(solution)/shard_map/ppermute | solution.py:351
  88.9 3.8 %combine.3.refs_0_ = bf16[16,6,64,128]{3,2,1,0:T(8,128)(2,1)} custom-call(s32[64]{0:T(128)} %plan.1, f32[5,6,128,128]{3,2,1,0:T(8,128)} %get-tuple-element.46.refs_0_, bf16[2,6,128,128]{3,2,1,0:T(8,128)(2,1)} %collective-permute-done.1.refs_1_, bf16[2,6,128,128]{3,2,1,0:T(8,128)(2,1)} %collective-permute-done.2.refs_2_, bf16[1,6,128,128]{3,2,1,0:T(8,128)(2,1)} %copy-done.18, ...), custom_call_target="tpu_custom_call" | custom-call | flops 1 | bytes 1024 | tf_op jit(solution)/shard_map/combine/pallas_call | solution.py:248
  93.5 6.5 %couple.8 = (f32[3,6,128,128]{3,2,1,0:T(8,128)}, bf16[1,6,128,128]{3,2,1,0:T(8,128)(2,1)}, bf16[1,6,128,128]{3,2,1,0:T(8,128)(2,1)}, bf16[1,6,128,128]{3,2,1,0:T(8,128)(2,1)}) custom-call(s32[64]{0:T(128)} %plan.1, s32[3]{0:T(128)} %pad_add_fusion.1.ids, bf16[240,240]{1,0:T(8,128)(2,1)} %maximum_maximum_fusion.table, ...), custom_call_target="tpu_custom_call" | custom-call | flops 1 | bytes 1024 | tf_op jit(solution)/shard_map/couple/pallas_call | solution.py:177
  100.7 1.0 collective-permute-done.16.refs_7_
  102.3 1.3 %add_convert_fusion.10 = (bf16[1,6,64,128]{3,2,1,0:T(8,128)(2,1)S(1)}, bf16[1,6,64,128]{3,2,1,0:T(8,128)(2,1)S(1)}, bf16[1,6,64,128]{3,2,1,0:T(8,128)(2,1)S(1)}) fusion(f32[3,6,128,128]{3,2,1,0:T(8,128)} %get-tuple-element.69.refs_6_, bf16[1,6,128,128]{3,2,1,0:T(8,128)(2,1)S(1)} %collective-permute-done.16.refs_7_, ...), kind=kLoop, calls=%fused_computation.15 | loop fusion | flops 442368 | bytes 1179648 | tf_op jit(solution)/shard_map/convert.2
  103.7 4.5 %couple.9 = (f32[2,6,128,128]{3,2,1,0:T(8,128)}, bf16[1,6,128,128]{3,2,1,0:T(8,128)(2,1)}, bf16[1,6,128,128]{3,2,1,0:T(8,128)(2,1)}) custom-call(s32[64]{0:T(128)} %plan.1, s32[3]{0:T(128)} %pad_add_fusion.1.ids, bf16[240,240]{1,0:T(8,128)(2,1)} %maximum_maximum_fusion.table, f32[6,2,360,128]{3,2,1,0:T(8,128)} %broadcast_in_dim.35.pots, ...), custom_call_target="tpu_custom_call" | custom-call | flops 1 | bytes 1024 | tf_op jit(solution)/shard_map/couple/pallas_call | solution.py:177
  108.5 4.3 %collective-permute-done.20.refs_10_ = bf16[3,6,64,128]{3,2,1,0:T(8,128)(2,1)S(1)} collective-permute-done((bf16[3,6,64,128]{3,2,1,0:T(8,128)(2,1)S(1)}, bf16[3,6,64,128]{3,2,1,0:T(8,128)(2,1)S(1)}, u32[]{:S(2)}, u32[]{:S(2)}) %collective-permute-start.20) | collective-permute-done | bytes 294944 | tf_op jit(solution)/shard_map/ppermute | solution.py:351
  112.8 1.6 %collective-permute-done.22.refs_3_ = bf16[1,6,128,128]{3,2,1,0:T(8,128)(2,1)S(1)} collective-permute-done((bf16[1,6,128,128]{3,2,1,0:T(8,128)(2,1)}, bf16[1,6,128,128]{3,2,1,0:T(8,128)(2,1)S(1)}, u32[]{:S(2)}, u32[]{:S(2)}) %collective-permute-start.22) | collective-permute-done | bytes 196640 | tf_op jit(solution)/shard_map/ppermute | solution.py:381
  114.4 1.1 add_convert_fusion.7
  116.0 3.5 %combine.4.refs_0_ = bf16[16,6,64,128]{3,2,1,0:T(8,128)(2,1)} custom-call(s32[64]{0:T(128)} %plan.1, bf16[16,6,64,128]{3,2,1,0:T(8,128)(2,1)} %combine.3.refs_0_, f32[5,6,128,128]{3,2,1,0:T(8,128)} %get-tuple-element.60.refs_1_, bf16[2,6,128,128]{3,2,1,0:T(8,128)(2,1)} %copy-done.4, ...), custom_call_target="tpu_custom_call", output_to_operand_aliasing={{}: (1, {})} | custom-call | flops 1 | bytes 1024 | tf_op jit(solution)/shard_map/combine/pallas_call | solution.py:248
  119.5 3.1 %collective-permute-done.23.refs_4_ = bf16[2,6,64,128]{3,2,1,0:T(8,128)(2,1)S(1)} collective-permute-done((bf16[2,6,64,128]{3,2,1,0:T(8,128)(2,1)S(1)}, bf16[2,6,64,128]{3,2,1,0:T(8,128)(2,1)S(1)}, u32[]{:S(2)}, u32[]{:S(2)}) %collective-permute-start.23) | collective-permute-done | bytes 196640 | tf_op jit(solution)/shard_map/ppermute | solution.py:351
  123.3 2.5 %combine.5 = bf16[16,6,64,128]{3,2,1,0:T(8,128)(2,1)} custom-call(s32[64]{0:T(128)} %plan.1, bf16[16,6,64,128]{3,2,1,0:T(8,128)(2,1)} %combine.4.refs_0_, f32[2,6,128,128]{3,2,1,0:T(8,128)} %get-tuple-element.79.refs_1_, bf16[1,6,128,128]{3,2,1,0:T(8,128)(2,1)} %copy-done.12, bf16[1,6,128,128]{3,2,1,0:T(8,128)(2,1)} %copy-done.13, ...), custom_call_target="tpu_custom_call", output_to_operand_aliasing={{}: (1, {})} | custom-call | flops 1 | bytes 1024 | tf_op jit(solution)/shard_map/combine/pallas_call | solution.py:248
  (112 shorter events, 11.9 us)
Async XLA Ops:
  5.5 22.4 %collective-permute-start.5 = (bf16[5,720,128]{2,1,0:T(8,128)(2,1)}, bf16[5,720,128]{2,1,0:T(8,128)(2,1)S(1)}, u32[]{:S(2)}, u32[]{:S(2)}) collective-permute-start(bf16[5,720,128]{2,1,0:T(8,128)(2,1)} %pick.4), channel_id=1, source_target_pairs={{0,4},{4,8},{8,12},{12,0},{1,5},{5,9},{9,13},{13,1},{2,6},{6,10},{... | collective-permute-start | bytes 2764808 | tf_op jit(solution)/shard_map/ppermute | solution.py:331
  7.2 4.4 %collective-permute-start = (f32[3,3,240]{2,1,0:T(4,128)S(1)}, f32[3,3,240]{2,1,0:T(4,128)S(1)}, u32[]{:S(2)}, u32[]{:S(2)}) collective-permute-start(f32[3,3,240]{2,1,0:T(4,128)S(1)} %bitcast.29), channel_id=1, source_target_pairs={{0,1},{1,0},{2,3},{3,2},{4,5},{5,4},{6,7},{7,6},{8,9},{9,8},{10,11... | collective-permute-start | bytes 25928 | tf_op jit(solution)/shard_map/ppermute | solution.py:308
  21.4 8.8 %collective-permute-start.3 = (bf16[1,6,128,128]{3,2,1,0:T(8,128)(2,1)}, bf16[1,6,128,128]{3,2,1,0:T(8,128)(2,1)S(1)}, u32[]{:S(2)}, u32[]{:S(2)}) collective-permute-start(bf16[1,6,128,128]{3,2,1,0:T(8,128)(2,1)} %get-tuple-element.49), channel_id=1, source_target_pairs={{0,1},{1,0},{2,3},{3,2},{4,5},{5,4},{6,7},{7,6},{8,9},{9,8},{10,11... | collective-permute-start | bytes 589832 | tf_op jit(solution)/shard_map/ppermute | solution.py:381
  21.9 8.4 %collective-permute-start.1 = (bf16[2,6,128,128]{3,2,1,0:T(8,128)(2,1)}, bf16[2,6,128,128]{3,2,1,0:T(8,128)(2,1)}, u32[]{:S(2)}, u32[]{:S(2)}) collective-permute-start(bf16[2,6,128,128]{3,2,1,0:T(8,128)(2,1)} %get-tuple-element.47), channel_id=1, source_target_pairs={{0,1},{1,0},{2,3},{3,2},{4,5},{5,4},{6,7},{7,6},{8,9},{9,8},{10,11... | collective-permute-start | bytes 1179656 | tf_op jit(solution)/shard_map/ppermute | solution.py:381
  22.0 8.3 %copy-start.1 = (f32[5,6,128,128]{3,2,1,0:T(8,128)S(1)}, f32[5,6,128,128]{3,2,1,0:T(8,128)}, u32[]{:S(2)}) copy-start(f32[5,6,128,128]{3,2,1,0:T(8,128)} %get-tuple-element.46.refs_0_) | copy-start | bytes 5898244
  22.0 8.3 %collective-permute-start.2 = (bf16[2,6,128,128]{3,2,1,0:T(8,128)(2,1)}, bf16[2,6,128,128]{3,2,1,0:T(8,128)(2,1)}, u32[]{:S(2)}, u32[]{:S(2)}) collective-permute-start(bf16[2,6,128,128]{3,2,1,0:T(8,128)(2,1)} %get-tuple-element.48), channel_id=1, source_target_pairs={{0,1},{1,0},{2,3},{3,2},{4,5},{5,4},{6,7},{7,6},{8,9},{9,8},{10,11... | collective-permute-start | bytes 1179656 | tf_op jit(solution)/shard_map/ppermute | solution.py:381
  27.9 35.3 %collective-permute-start.10 = (bf16[5,720,128]{2,1,0:T(8,128)(2,1)}, bf16[5,720,128]{2,1,0:T(8,128)(2,1)S(1)}, u32[]{:S(2)}, u32[]{:S(2)}) collective-permute-start(bf16[5,720,128]{2,1,0:T(8,128)(2,1)} %pick.6), channel_id=1, source_target_pairs={{0,12},{4,0},{8,4},{12,8},{1,13},{5,1},{9,5},{13,9},{2,14},{6,2},{... | collective-permute-start | bytes 2764808 | tf_op jit(solution)/shard_map/ppermute | solution.py:331
  30.2 11.3 %copy-start.18 = (bf16[1,6,128,128]{3,2,1,0:T(8,128)(2,1)}, bf16[1,6,128,128]{3,2,1,0:T(8,128)(2,1)S(1)}, u32[]{:S(2)}) copy-start(bf16[1,6,128,128]{3,2,1,0:T(8,128)(2,1)S(1)} %collective-permute-done.3.refs_3_) | copy-start | bytes 589828
  32.3 31.0 %collective-permute-start.4 = (bf16[5,6,64,128]{3,2,1,0:T(8,128)(2,1)}, bf16[5,6,64,128]{3,2,1,0:T(8,128)(2,1)S(1)}, u32[]{:S(2)}, u32[]{:S(2)}) collective-permute-start(bf16[5,6,64,128]{3,2,1,0:T(8,128)(2,1)} %pad_maximum_fusion), channel_id=1, source_target_pairs={{0,2},{2,0},{1,3},{3,1},{4,6},{6,4},{5,7},{7,5},{8,10},{10,8},{9,1... | collective-permute-start | bytes 1474568 | tf_op jit(solution)/shard_map/ppermute | solution.py:351
  41.6 1.7 %collective-permute-start.8 = (bf16[1,6,128,128]{3,2,1,0:T(8,128)(2,1)}, bf16[1,6,128,128]{3,2,1,0:T(8,128)(2,1)S(1)}, u32[]{:S(2)}, u32[]{:S(2)}) collective-permute-start(bf16[1,6,128,128]{3,2,1,0:T(8,128)(2,1)} %get-tuple-element.55), channel_id=1, source_target_pairs={{0,1},{1,0},{2,3},{3,2},{4,5},{5,4},{6,7},{7,6},{8,9},{9,8},{10,11... | collective-permute-start | bytes 589832 | tf_op jit(solution)/shard_map/ppermute | solution.py:381
  41.7 21.6 %collective-permute-start.6 = (bf16[2,6,128,128]{3,2,1,0:T(8,128)(2,1)}, bf16[2,6,128,128]{3,2,1,0:T(8,128)(2,1)S(1)}, u32[]{:S(2)}, u32[]{:S(2)}) collective-permute-start(bf16[2,6,128,128]{3,2,1,0:T(8,128)(2,1)} %get-tuple-element.53), channel_id=1, source_target_pairs={{0,1},{1,0},{2,3},{3,2},{4,5},{5,4},{6,7},{7,6},{8,9},{9,8},{10,11... | collective-permute-start | bytes 1179656 | tf_op jit(solution)/shard_map/ppermute | solution.py:381
  42.2 21.1 %collective-permute-start.7 = (bf16[2,6,128,128]{3,2,1,0:T(8,128)(2,1)}, bf16[2,6,128,128]{3,2,1,0:T(8,128)(2,1)S(1)}, u32[]{:S(2)}, u32[]{:S(2)}) collective-permute-start(bf16[2,6,128,128]{3,2,1,0:T(8,128)(2,1)} %get-tuple-element.54), channel_id=1, source_target_pairs={{0,1},{1,0},{2,3},{3,2},{4,5},{5,4},{6,7},{7,6},{8,9},{9,8},{10,11... | collective-permute-start | bytes 1179656 | tf_op jit(solution)/shard_map/ppermute | solution.py:381
  43.3 28.7 %copy-start.19 = (bf16[1,6,128,128]{3,2,1,0:T(8,128)(2,1)}, bf16[1,6,128,128]{3,2,1,0:T(8,128)(2,1)S(1)}, u32[]{:S(2)}) copy-start(bf16[1,6,128,128]{3,2,1,0:T(8,128)(2,1)S(1)} %collective-permute-done.8.refs_8_) | copy-start | bytes 589828
  43.3 49.4 %collective-permute-start.15 = (bf16[3,720,128]{2,1,0:T(8,128)(2,1)}, bf16[3,720,128]{2,1,0:T(8,128)(2,1)S(1)}, u32[]{:S(2)}, u32[]{:S(2)}) collective-permute-start(bf16[3,720,128]{2,1,0:T(8,128)(2,1)} %pick.5), channel_id=1, source_target_pairs={{0,8},{4,12},{8,0},{12,4},{1,9},{5,13},{9,1},{13,5},{2,10},{6,14},... | collective-permute-start | bytes 1658888 | tf_op jit(solution)/shard_map/ppermute | solution.py:331
  63.3 9.4 %copy-start.6 = (bf16[2,6,128,128]{3,2,1,0:T(8,128)(2,1)}, bf16[2,6,128,128]{3,2,1,0:T(8,128)(2,1)S(1)}, u32[]{:S(2)}) copy-start(bf16[2,6,128,128]{3,2,1,0:T(8,128)(2,1)S(1)} %collective-permute-done.6.refs_6_) | copy-start | bytes 1179652
  63.3 9.4 %copy-start.7 = (bf16[2,6,128,128]{3,2,1,0:T(8,128)(2,1)}, bf16[2,6,128,128]{3,2,1,0:T(8,128)(2,1)S(1)}, u32[]{:S(2)}) copy-start(bf16[2,6,128,128]{3,2,1,0:T(8,128)(2,1)S(1)} %collective-permute-done.7.refs_7_) | copy-start | bytes 1179652
  64.2 7.9 %copy-start.10 = (bf16[5,6,64,128]{3,2,1,0:T(8,128)(2,1)}, bf16[5,6,64,128]{3,2,1,0:T(8,128)(2,1)S(1)}, u32[]{:S(2)}) copy-start(bf16[5,6,64,128]{3,2,1,0:T(8,128)(2,1)S(1)} %collective-permute-done.4.refs_4_) | copy-start | bytes 1474564
  72.0 2.9 %collective-permute-start.11 = (bf16[2,6,128,128]{3,2,1,0:T(8,128)(2,1)}, bf16[2,6,128,128]{3,2,1,0:T(8,128)(2,1)S(1)}, u32[]{:S(2)}, u32[]{:S(2)}) collective-permute-start(bf16[2,6,128,128]{3,2,1,0:T(8,128)(2,1)} %get-tuple-element.61), channel_id=1, source_target_pairs={{0,1},{1,0},{2,3},{3,2},{4,5},{5,4},{6,7},{7,6},{8,9},{9,8},{10,11... | collective-permute-start | bytes 1179656 | tf_op jit(solution)/shard_map/ppermute | solution.py:381
  72.1 2.8 %collective-permute-start.12 = (bf16[2,6,128,128]{3,2,1,0:T(8,128)(2,1)}, bf16[2,6,128,128]{3,2,1,0:T(8,128)(2,1)S(1)}, u32[]{:S(2)}, u32[]{:S(2)}) collective-permute-start(bf16[2,6,128,128]{3,2,1,0:T(8,128)(2,1)} %get-tuple-element.62), channel_id=1, source_target_pairs={{0,1},{1,0},{2,3},{3,2},{4,5},{5,4},{6,7},{7,6},{8,9},{9,8},{10,11... | collective-permute-start | bytes 1179656 | tf_op jit(solution)/shard_map/ppermute | solution.py:381
  72.6 2.3 %collective-permute-start.13 = (bf16[1,6,128,128]{3,2,1,0:T(8,128)(2,1)}, bf16[1,6,128,128]{3,2,1,0:T(8,128)(2,1)S(1)}, u32[]{:S(2)}, u32[]{:S(2)}) collective-permute-start(bf16[1,6,128,128]{3,2,1,0:T(8,128)(2,1)} %get-tuple-element.63), channel_id=1, source_target_pairs={{0,1},{1,0},{2,3},{3,2},{4,5},{5,4},{6,7},{7,6},{8,9},{9,8},{10,11... | collective-permute-start | bytes 589832 | tf_op jit(solution)/shard_map/ppermute | solution.py:381
  74.0 14.1 %collective-permute-start.9 = (bf16[5,6,64,128]{3,2,1,0:T(8,128)(2,1)S(1)}, bf16[5,6,64,128]{3,2,1,0:T(8,128)(2,1)S(1)}, u32[]{:S(2)}, u32[]{:S(2)}) collective-permute-start(bf16[5,6,64,128]{3,2,1,0:T(8,128)(2,1)S(1)} %pad_maximum_fusion.1), channel_id=1, source_target_pairs={{0,2},{2,0},{1,3},{3,1},{4,6},{6,4},{5,7},{7,5},{8,10},{10,8},{9,1... | collective-permute-start | bytes 1474568 | tf_op jit(solution)/shard_map/ppermute | solution.py:351
  75.2 25.4 %collective-permute-start.14 = (bf16[5,6,64,128]{3,2,1,0:T(8,128)(2,1)S(1)}, bf16[5,6,64,128]{3,2,1,0:T(8,128)(2,1)S(1)}, u32[]{:S(2)}, u32[]{:S(2)}) collective-permute-start(bf16[5,6,64,128]{3,2,1,0:T(8,128)(2,1)S(1)} %pad_maximum_fusion.2), channel_id=1, source_target_pairs={{0,2},{2,0},{1,3},{3,1},{4,6},{6,4},{5,7},{7,5},{8,10},{10,8},{9,1... | collective-permute-start | bytes 1474568 | tf_op jit(solution)/shard_map/ppermute | solution.py:351
  78.9 21.6 %collective-permute-start.18 = (bf16[2,720,128]{2,1,0:T(8,128)(2,1)}, bf16[2,720,128]{2,1,0:T(8,128)(2,1)}, u32[]{:S(2)}, u32[]{:S(2)}) collective-permute-start(bf16[2,720,128]{2,1,0:T(8,128)(2,1)} %pick.7), channel_id=1, source_target_pairs={{0,8},{4,12},{8,0},{12,4},{1,9},{5,13},{9,1},{13,5},{2,10},{6,14},... | collective-permute-start | bytes 1105928 | tf_op jit(solution)/shard_map/ppermute | solution.py:331
  100.0 1.7 %collective-permute-start.16 = (bf16[1,6,128,128]{3,2,1,0:T(8,128)(2,1)}, bf16[1,6,128,128]{3,2,1,0:T(8,128)(2,1)S(1)}, u32[]{:S(2)}, u32[]{:S(2)}) collective-permute-start(bf16[1,6,128,128]{3,2,1,0:T(8,128)(2,1)} %get-tuple-element.70), channel_id=1, source_target_pairs={{0,1},{1,0},{2,3},{3,2},{4,5},{5,4},{6,7},{7,6},{8,9},{9,8},{10,11... | collective-permute-start | bytes 589832 | tf_op jit(solution)/shard_map/ppermute | solution.py:381
  100.0 1.9 %collective-permute-start.17 = (bf16[1,6,128,128]{3,2,1,0:T(8,128)(2,1)}, bf16[1,6,128,128]{3,2,1,0:T(8,128)(2,1)S(1)}, u32[]{:S(2)}, u32[]{:S(2)}) collective-permute-start(bf16[1,6,128,128]{3,2,1,0:T(8,128)(2,1)} %get-tuple-element.71), channel_id=1, source_target_pairs={{0,1},{1,0},{2,3},{3,2},{4,5},{5,4},{6,7},{7,6},{8,9},{9,8},{10,11... | collective-permute-start | bytes 589832 | tf_op jit(solution)/shard_map/ppermute | solution.py:381
  100.5 7.7 %copy-start.9 = (bf16[5,6,64,128]{3,2,1,0:T(8,128)(2,1)}, bf16[5,6,64,128]{3,2,1,0:T(8,128)(2,1)S(1)}, u32[]{:S(2)}) copy-start(bf16[5,6,64,128]{3,2,1,0:T(8,128)(2,1)S(1)} %collective-permute-done.14.refs_5_) | copy-start | bytes 1474564
  100.5 1.7 %collective-permute-start.19 = (bf16[1,6,128,128]{3,2,1,0:T(8,128)(2,1)}, bf16[1,6,128,128]{3,2,1,0:T(8,128)(2,1)S(1)}, u32[]{:S(2)}, u32[]{:S(2)}) collective-permute-start(bf16[1,6,128,128]{3,2,1,0:T(8,128)(2,1)} %get-tuple-element.75), channel_id=1, source_target_pairs={{0,1},{1,0},{2,3},{3,2},{4,5},{5,4},{6,7},{7,6},{8,9},{9,8},{10,11... | collective-permute-start | bytes 589832 | tf_op jit(solution)/shard_map/ppermute | solution.py:381
  103.6 9.2 %collective-permute-start.20 = (bf16[3,6,64,128]{3,2,1,0:T(8,128)(2,1)S(1)}, bf16[3,6,64,128]{3,2,1,0:T(8,128)(2,1)S(1)}, u32[]{:S(2)}, u32[]{:S(2)}) collective-permute-start(bf16[3,6,64,128]{3,2,1,0:T(8,128)(2,1)S(1)} %pad_maximum_fusion.3), channel_id=1, source_target_pairs={{0,2},{2,0},{1,3},{3,1},{4,6},{6,4},{5,7},{7,5},{8,10},{10,8},{9,1... | collective-permute-start | bytes 884744 | tf_op jit(solution)/shard_map/ppermute | solution.py:351
  108.3 4.5 %collective-permute-start.21 = (bf16[1,6,128,128]{3,2,1,0:T(8,128)(2,1)}, bf16[1,6,128,128]{3,2,1,0:T(8,128)(2,1)S(1)}, u32[]{:S(2)}, u32[]{:S(2)}) collective-permute-start(bf16[1,6,128,128]{3,2,1,0:T(8,128)(2,1)} %get-tuple-element.80), channel_id=1, source_target_pairs={{0,1},{1,0},{2,3},{3,2},{4,5},{5,4},{6,7},{7,6},{8,9},{9,8},{10,11... | collective-permute-start | bytes 589832 | tf_op jit(solution)/shard_map/ppermute | solution.py:381
  112.8 1.7 %collective-permute-start.22 = (bf16[1,6,128,128]{3,2,1,0:T(8,128)(2,1)}, bf16[1,6,128,128]{3,2,1,0:T(8,128)(2,1)S(1)}, u32[]{:S(2)}, u32[]{:S(2)}) collective-permute-start(bf16[1,6,128,128]{3,2,1,0:T(8,128)(2,1)} %get-tuple-element.82), channel_id=1, source_target_pairs={{0,1},{1,0},{2,3},{3,2},{4,5},{5,4},{6,7},{7,6},{8,9},{9,8},{10,11... | collective-permute-start | bytes 589832 | tf_op jit(solution)/shard_map/ppermute | solution.py:381
  112.8 6.7 %copy-start.12 = (bf16[1,6,128,128]{3,2,1,0:T(8,128)(2,1)}, bf16[1,6,128,128]{3,2,1,0:T(8,128)(2,1)S(1)}, u32[]{:S(2)}) copy-start(bf16[1,6,128,128]{3,2,1,0:T(8,128)(2,1)S(1)} %collective-permute-done.21.refs_2_) | copy-start | bytes 589828
  115.6 7.0 %collective-permute-start.23 = (bf16[2,6,64,128]{3,2,1,0:T(8,128)(2,1)S(1)}, bf16[2,6,64,128]{3,2,1,0:T(8,128)(2,1)S(1)}, u32[]{:S(2)}, u32[]{:S(2)}) collective-permute-start(bf16[2,6,64,128]{3,2,1,0:T(8,128)(2,1)S(1)} %pad_maximum_fusion.4), channel_id=1, source_target_pairs={{0,2},{2,0},{1,3},{3,1},{4,6},{6,4},{5,7},{7,5},{8,10},{10,8},{9,1... | collective-permute-start | bytes 589832 | tf_op jit(solution)/shard_map/ppermute | solution.py:351
  (16 other events, 59.8 us)
